TPU v7x, 128 devices: a whole 4x4x4 slice. The times are simulated.
128 devices in a mesh: dp: 2 (over z_lo), outer: 4 (over y), inner: 16 (over z_hi, x, core).
Axes of the slice: x: 4, y: 4, z: 4 (z_hi: 2, z_lo: 2; z = z_hi * 2 + z_lo), core: 2. Of those that a mesh axis runs over, the one named last changes fastest.
Arguments:
- query_gate: bfloat16 [65536, 256], P(('dp', 'outer', 'inner')), parts along dimension 0, may hold values from -6 to 6
- key_gate: bfloat16 [65536, 256], P(('dp', 'outer', 'inner')), parts along dimension 0, may hold values from -6 to 6
- value_seq: bfloat16 [65536, 256], P(('dp', 'outer', 'inner')), parts along dimension 0, may hold values from -6 to 6
- grad_output: bfloat16 [65536, 256], P(('dp', 'outer', 'inner')), parts along dimension 0, may hold values from -6 to 6
- filter_taps: float32 [32768, 256], P(('outer', 'inner')), may hold values from -2 to 2
Outputs:
- grad_query: bfloat16 [65536, 256], P(('dp', 'outer', 'inner')), parts along dimension 0
- grad_key: bfloat16 [65536, 256], P(('dp', 'outer', 'inner')), parts along dimension 0
- grad_value: bfloat16 [65536, 256], P(('dp', 'outer', 'inner')), parts along dimension 0
- grad_filter: float32 [65536, 256], P(('dp', 'outer', 'inner')), parts along dimension 0
There are 2 independent parts, one for each index of `dp`. A program takes and returns all parts, laid end to end along the dimension named above; an argument that names none is the same for every part. Nothing has to cross between parts.
All inputs are finite; a program needn't handle non-finite values.
Results may differ from a plain program's by a relative error of at most 0.0025.
Values sent between devices are 32-bit elements; how exact they have to be, the bound alone decides.
No kernel may reach another device: no remote copies, remote signals or barrier semaphores. Data moves between devices by JAX's collectives and lax.ppermute only.
A program may use at most 128 MiB of HBM per device.

v0:
```python
import functools
import math

import jax
import jax.numpy as jnp
import numpy as np
from jax import lax
from jax.experimental import pallas as pl
from jax.experimental.pallas import tpu as pltpu
from jax.sharding import PartitionSpec as P

AXES = ("outer", "inner")
LANES = 128
SIGNALS = 3


def split_table(table):
    table = np.asarray(table, np.float32)
    high = table.astype(jnp.bfloat16)
    low = (table - high.astype(np.float32)).astype(jnp.bfloat16)
    return high, low


def tables(groups, width):
    pieces = width // LANES
    n1 = groups * pieces
    length = n1 * LANES
    order = (np.arange(groups)[None, :] * pieces + np.arange(pieces)[:, None]).reshape(-1)
    k1 = np.arange(n1) + 0.25
    turn = (k1[:, None] * order[None, :]) * (2.0 * math.pi / n1)
    outer = np.concatenate([np.cos(turn), -np.sin(turn)], axis=0)
    back_outer = np.concatenate([np.cos(turn.T), -np.sin(turn.T)], axis=1) / length
    twist = k1[:, None] * np.arange(LANES)[None, :] * (2.0 * math.pi / length)
    lane = np.arange(LANES)
    spin = lane[:, None] * lane[None, :] * (2.0 * math.pi / LANES)
    cos, sin = np.cos(spin), np.sin(spin)
    inner = np.block([[cos, -sin], [sin, cos]])
    back_inner = np.block([[cos, sin], [-sin, cos]])
    return (
        split_table(outer),
        split_table(inner),
        split_table(back_outer),
        split_table(back_inner),
        np.cos(twist).astype(np.float32),
        np.sin(twist).astype(np.float32),
    )


def split(value):
    high = value.astype(jnp.bfloat16)
    low = (value - high.astype(jnp.float32)).astype(jnp.bfloat16)
    return high, low


def dot3(left, right):
    dot = functools.partial(jnp.dot, preferred_element_type=jnp.float32)
    return dot(left[0], right[0]) + (dot(left[0], right[1]) + dot(left[1], right[0]))


def pack_kernel(groups, key_ref, value_ref, grad_ref, query_ref, taps_ref, out_ref):
    rows, channels = key_ref.shape
    pieces, per = rows // LANES, channels // groups
    slab = SIGNALS * per * pieces
    for piece in range(pieces):
        span = slice(piece * LANES, (piece + 1) * LANES)
        mixed = key_ref[span, :].astype(jnp.float32) * value_ref[span, :].astype(jnp.float32)
        grad = grad_ref[span, :].astype(jnp.float32) * query_ref[span, :].astype(jnp.float32)
        for s, signal in enumerate((mixed, grad, taps_ref[span, :])):
            turned = signal.T
            for c in range(per):
                row = (s * per + c) * pieces + piece
                out_ref[pl.ds(row, groups, stride=slab), :] = turned[c * groups : (c + 1) * groups, :]


def unpack_kernel(groups, in_ref, key_ref, value_ref, grad_ref, gq_ref, gk_ref, gv_ref, gf_ref):
    rows, channels = key_ref.shape
    pieces, per = rows // LANES, channels // groups
    slab = SIGNALS * per * pieces
    scale = 1.0 / math.sqrt(groups * rows)

    def signal(s, piece):
        parts = [
            in_ref[pl.ds((s * per + c) * pieces + piece, groups, stride=slab), :] for c in range(per)
        ]
        return jnp.concatenate(parts, axis=0).T

    for piece in range(pieces):
        span = slice(piece * LANES, (piece + 1) * LANES)
        gq_ref[span, :] = (grad_ref[span, :].astype(jnp.float32) * signal(0, piece)).astype(gq_ref.dtype)
        corr = signal(1, piece)
        gk_ref[span, :] = (corr * value_ref[span, :].astype(jnp.float32)).astype(gk_ref.dtype)
        gv_ref[span, :] = (corr * key_ref[span, :].astype(jnp.float32)).astype(gv_ref.dtype)
        gf_ref[span, :] = signal(2, piece) * scale


def convolve_kernel(
    groups, per, in_ref, outer_hi, outer_lo, inner_hi, inner_lo,
    back_outer_hi, back_outer_lo, back_inner_hi, back_inner_lo, cos_ref, sin_ref, out_ref,
):
    n1 = cos_ref.shape[0]
    pieces = n1 // groups
    slab = SIGNALS * per * pieces
    outer = (outer_hi[...], outer_lo[...])
    inner = (inner_hi[...], inner_lo[...])
    back_outer = (back_outer_hi[...], back_outer_lo[...])
    back_inner = (back_inner_hi[...], back_inner_lo[...])

    def load(s, c):
        parts = [
            in_ref[pl.ds((s * per + c) * pieces + piece, groups, stride=slab), :]
            for piece in range(pieces)
        ]
        return jnp.concatenate(parts, axis=0)

    def forward(s, c):
        pair = jnp.concatenate([load(s, c), load(s, c + 1)], axis=1)
        mixed = dot3(outer, split(pair))
        spectra = []
        for half in range(2):
            lanes = slice(half * LANES, (half + 1) * LANES)
            re, im = mixed[:n1, lanes], mixed[n1:, lanes]
            cos, sin = cos_ref[...], sin_ref[...]
            turned = jnp.concatenate([re * cos + im * sin, im * cos - re * sin], axis=1)
            done = dot3(split(turned), inner)
            spectra.append((done[:, :LANES], done[:, LANES:]))
        return spectra

    def product(left, right, sign):
        left_re, left_im = left[0], sign * left[1]
        re = left_re * right[0] - left_im * right[1]
        im = left_re * right[1] + left_im * right[0]
        return jnp.concatenate([re, im], axis=1)

    def inverse(s, c, spectra):
        columns = []
        for spectrum in spectra:
            done = dot3(split(spectrum), back_inner)
            re, im = done[:, :LANES], done[:, LANES:]
            cos, sin = cos_ref[...], sin_ref[...]
            columns.append(jnp.concatenate([re * cos - im * sin, re * sin + im * cos], axis=0))
        pair = dot3(back_outer, split(jnp.concatenate(columns, axis=1)))
        for half in range(2):
            for piece in range(pieces):
                row = (s * per + c + half) * pieces + piece
                block = pair[piece * groups : (piece + 1) * groups, half * LANES : (half + 1) * LANES]
                out_ref[pl.ds(row, groups, stride=slab), :] = block

    for c in range(0, per, 2):
        mixed, grad, taps = forward(0, c), forward(1, c), forward(2, c)
        inverse(0, c, [product(t, m, 1.0) for t, m in zip(taps, mixed)])
        inverse(1, c, [product(t, g, -1.0) for t, g in zip(taps, grad)])
        inverse(2, c, [product(m, g, -1.0) for m, g in zip(mixed, grad)])


def params(size):
    return pltpu.CompilerParams(vmem_limit_bytes=size << 20)


def exchange(slabs, groups):
    slabs = slabs.reshape(groups, -1, LANES)
    slabs = lax.all_to_all(slabs, AXES, split_axis=0, concat_axis=0, tiled=True)
    return slabs.reshape(-1, LANES)


def per_device(query_gate, key_gate, value_seq, grad_output, filter_taps):
    groups = lax.axis_size(AXES)
    rows, channels = query_gate.shape
    per = channels // groups
    flat = jax.ShapeDtypeStruct((SIGNALS * channels * rows // LANES, LANES), jnp.float32)
    outer, inner, back_outer, back_inner, cos, sin = tables(groups, rows)

    packed = pl.pallas_call(
        functools.partial(pack_kernel, groups), out_shape=flat, compiler_params=params(32), name="pack"
    )(key_gate, value_seq, grad_output, query_gate, filter_taps)
    received = exchange(packed, groups)
    results = pl.pallas_call(
        functools.partial(convolve_kernel, groups, per), out_shape=flat, compiler_params=params(48), name="convolve"
    )(received, *outer, *inner, *back_outer, *back_inner, cos, sin)
    returned = exchange(results, groups)
    narrow = jax.ShapeDtypeStruct((rows, channels), jnp.bfloat16)
    wide = jax.ShapeDtypeStruct((rows, channels), jnp.float32)
    return pl.pallas_call(
        functools.partial(unpack_kernel, groups),
        out_shape=(narrow, narrow, narrow, wide),
        compiler_params=params(32),
        name="unpack",
    )(returned, key_gate, value_seq, grad_output)


def solution(mesh):
    split_rows = P(("dp",) + AXES, None)
    return jax.shard_map(
        per_device,
        mesh=mesh,
        in_specs=(split_rows, split_rows, split_rows, split_rows, P(AXES, None)),
        out_specs=(split_rows, split_rows, split_rows, split_rows),
        check_vma=False,
    )
```

profile of v0, /device:TPU:1, one launch (start us, length us, event | category | flops | bytes accessed | tf_op | source)
XLA Modules:
  0.0 81.8 jit_solution(15535741785997472696)
XLA Ops:
  0.6 0.0 copy-start
  0.6 0.9 %copy-done = bf16[512,256]{1,0:T(8,128)(2,1)S(1)} copy-done((bf16[512,256]{1,0:T(8,128)(2,1)S(1)}, bf16[512,256]{1,0:T(8,128)(2,1)}, u32[]{:S(2)}) %copy-start) | copy-done | bytes 262168
  1.6 0.9 %copy-done.2 = bf16[512,256]{1,0:T(8,128)(2,1)S(1)} copy-done((bf16[512,256]{1,0:T(8,128)(2,1)S(1)}, bf16[512,256]{1,0:T(8,128)(2,1)}, u32[]{:S(2)}) %copy-start.2) | copy-done | bytes 262168
  2.5 0.9 %copy-done.4 = bf16[512,256]{1,0:T(8,128)(2,1)S(1)} copy-done((bf16[512,256]{1,0:T(8,128)(2,1)S(1)}, bf16[512,256]{1,0:T(8,128)(2,1)}, u32[]{:S(2)}) %copy-start.4) | copy-done | bytes 262168
  3.5 1.0 %copy-done.6 = f32[512,256]{1,0:T(8,128)S(1)} copy-done((f32[512,256]{1,0:T(8,128)S(1)}, f32[512,256]{1,0:T(8,128)}, u32[]{:S(2)}) %copy-start.6) | copy-done | bytes 524312
  4.5 0.9 %copy-done.7 = bf16[512,256]{1,0:T(8,128)(2,1)S(1)} copy-done((bf16[512,256]{1,0:T(8,128)(2,1)S(1)}, bf16[512,256]{1,0:T(8,128)(2,1)}, u32[]{:S(2)}) %copy-start.7) | copy-done | bytes 262168
  5.5 0.6 pack.1
  6.1 0.0 copy-start.8
  6.1 0.0 copy-start.9
  6.1 0.0 copy-start.10
  6.1 0.0 copy-start.11
  6.1 0.0 copy-start.12
  6.1 0.0 copy-start.13
  6.1 0.0 copy-start.14
  6.2 0.0 copy-start.15
  6.2 0.0 copy-start.16
  6.2 0.0 copy-start.17
  6.2 37.2 %all_to_all.10 = f32[64,48,128]{2,1,0:T(8,128)S(1)} all-to-all(f32[64,48,128]{2,1,0:T(8,128)S(1)} %bitcast.7), channel_id=1, replica_groups=mesh['dp'=2,'outer'=4,'inner'=16] {'outer','inner'}, dimensions={0} | all-to-all | bytes 3145728 | tf_op jit(solution)/shard_map/all_to_all | solution.py:161
  43.5 6.8 %convolve.1 = f32[3072,128]{1,0:T(8,128)S(1)} custom-call(f32[3072,128]{1,0:T(8,128)S(1)} %bitcast.4, bf16[512,256]{1,0:T(8,128)(2,1)S(1)} %copy-done.11, bf16[512,256]{1,0:T(8,128)(2,1)S(1)} %copy-done.10, bf16[256,256]{1,0:T(8,128)(2,1)S(1)} %copy-done.17, bf16[256,256]{1,0:T(8,128)(2,1)S(1)} %copy-done.16, bf16[256,512]{1,0:T(8,128)(2,1)S(1)} %copy-done.9, ...), custom_call_target="tpu_custom_call" | custom-call | tf_op jit(solution)/shard_map/convolve/pallas_call | solution.py:176
  50.4 0.0 copy-start.1
  50.4 0.0 copy-start.3
  50.4 0.0 copy-start.5
  50.4 29.9 %all_to_all.11 = f32[64,48,128]{2,1,0:T(8,128)S(1)} all-to-all(f32[64,48,128]{2,1,0:T(8,128)S(1)} %bitcast.5), channel_id=1, replica_groups=mesh['dp'=2,'outer'=4,'inner'=16] {'outer','inner'}, dimensions={0} | all-to-all | bytes 3145728 | tf_op jit(solution)/shard_map/all_to_all | solution.py:161
  80.3 1.5 %unpack.1 = (bf16[512,256]{1,0:T(8,128)(2,1)}, bf16[512,256]{1,0:T(8,128)(2,1)}, bf16[512,256]{1,0:T(8,128)(2,1)}, f32[512,256]{1,0:T(8,128)}) custom-call(f32[3072,128]{1,0:T(8,128)S(1)} %bitcast.6, bf16[512,256]{1,0:T(8,128)(2,1)S(1)} %copy-done.1, bf16[512,256]{1,0:T(8,128)(2,1)S(1)} %copy-done.3, bf16[512,256]{1,0:T(8,128)(2,1)S(1)} %copy-done.5), custom_call_target="tpu_custom_call" | custom-call | tf_op jit(solution)/shard_map/unpack/pallas_call | solution.py:182
  (17 shorter events, 0.0 us)
Async XLA Ops:
  0.6 1.0 %copy-start = (bf16[512,256]{1,0:T(8,128)(2,1)S(1)}, bf16[512,256]{1,0:T(8,128)(2,1)}, u32[]{:S(2)}) copy-start(bf16[512,256]{1,0:T(8,128)(2,1)} %key_ref.3) | copy-start | bytes 786436
  1.6 0.9 %copy-start.2 = (bf16[512,256]{1,0:T(8,128)(2,1)S(1)}, bf16[512,256]{1,0:T(8,128)(2,1)}, u32[]{:S(2)}) copy-start(bf16[512,256]{1,0:T(8,128)(2,1)} %value_ref.3) | copy-start | bytes 786436
  2.5 0.9 %copy-start.4 = (bf16[512,256]{1,0:T(8,128)(2,1)S(1)}, bf16[512,256]{1,0:T(8,128)(2,1)}, u32[]{:S(2)}) copy-start(bf16[512,256]{1,0:T(8,128)(2,1)} %grad_ref.3) | copy-start | bytes 786436
  3.5 1.0 %copy-start.6 = (f32[512,256]{1,0:T(8,128)S(1)}, f32[512,256]{1,0:T(8,128)}, u32[]{:S(2)}) copy-start(f32[512,256]{1,0:T(8,128)} %taps_ref.1) | copy-start | bytes 1572868
  4.5 0.9 %copy-start.7 = (bf16[512,256]{1,0:T(8,128)(2,1)S(1)}, bf16[512,256]{1,0:T(8,128)(2,1)}, u32[]{:S(2)}) copy-start(bf16[512,256]{1,0:T(8,128)(2,1)} %query_ref.1) | copy-start | bytes 786436
  6.1 37.4 %copy-start.8 = (bf16[256,512]{1,0:T(8,128)(2,1)S(1)}, bf16[256,512]{1,0:T(8,128)(2,1)}, u32[]{:S(2)}) copy-start(bf16[256,512]{1,0:T(8,128)(2,1)} %constant.25.clone.back_outer_lo) | copy-start | bytes 786436
  6.1 37.4 %copy-start.9 = (bf16[256,512]{1,0:T(8,128)(2,1)S(1)}, bf16[256,512]{1,0:T(8,128)(2,1)}, u32[]{:S(2)}) copy-start(bf16[256,512]{1,0:T(8,128)(2,1)} %constant.24.clone.back_outer_hi) | copy-start | bytes 786436
  6.1 37.4 %copy-start.10 = (bf16[512,256]{1,0:T(8,128)(2,1)S(1)}, bf16[512,256]{1,0:T(8,128)(2,1)}, u32[]{:S(2)}) copy-start(bf16[512,256]{1,0:T(8,128)(2,1)} %constant.21.clone.outer_lo) | copy-start | bytes 786436
  6.1 37.3 %copy-start.11 = (bf16[512,256]{1,0:T(8,128)(2,1)S(1)}, bf16[512,256]{1,0:T(8,128)(2,1)}, u32[]{:S(2)}) copy-start(bf16[512,256]{1,0:T(8,128)(2,1)} %constant.20.clone.outer_hi) | copy-start | bytes 786436
  6.1 37.3 %copy-start.12 = (f32[256,128]{1,0:T(8,128)S(1)}, f32[256,128]{1,0:T(8,128)}, u32[]{:S(2)}) copy-start(f32[256,128]{1,0:T(8,128)} %constant.29.clone.sin_ref) | copy-start | bytes 393220
  6.1 37.3 %copy-start.13 = (f32[256,128]{1,0:T(8,128)S(1)}, f32[256,128]{1,0:T(8,128)}, u32[]{:S(2)}) copy-start(f32[256,128]{1,0:T(8,128)} %constant.28.clone.cos_ref) | copy-start | bytes 393220
  6.1 37.3 %copy-start.14 = (bf16[256,256]{1,0:T(8,128)(2,1)S(1)}, bf16[256,256]{1,0:T(8,128)(2,1)}, u32[]{:S(2)}) copy-start(bf16[256,256]{1,0:T(8,128)(2,1)} %constant.27.clone.back_inner_lo) | copy-start | bytes 393220
  6.2 37.3 %copy-start.15 = (bf16[256,256]{1,0:T(8,128)(2,1)S(1)}, bf16[256,256]{1,0:T(8,128)(2,1)}, u32[]{:S(2)}) copy-start(bf16[256,256]{1,0:T(8,128)(2,1)} %constant.26.clone.back_inner_hi) | copy-start | bytes 393220
  6.2 37.3 %copy-start.16 = (bf16[256,256]{1,0:T(8,128)(2,1)S(1)}, bf16[256,256]{1,0:T(8,128)(2,1)}, u32[]{:S(2)}) copy-start(bf16[256,256]{1,0:T(8,128)(2,1)} %constant.23.clone.inner_lo) | copy-start | bytes 393220
  6.2 37.3 %copy-start.17 = (bf16[256,256]{1,0:T(8,128)(2,1)S(1)}, bf16[256,256]{1,0:T(8,128)(2,1)}, u32[]{:S(2)}) copy-start(bf16[256,256]{1,0:T(8,128)(2,1)} %constant.22.clone.inner_hi) | copy-start | bytes 393220
  50.4 29.9 %copy-start.1 = (bf16[512,256]{1,0:T(8,128)(2,1)S(1)}, bf16[512,256]{1,0:T(8,128)(2,1)}, u32[]{:S(2)}) copy-start(bf16[512,256]{1,0:T(8,128)(2,1)} %key_ref.3) | copy-start | bytes 786436
  50.4 29.9 %copy-start.3 = (bf16[512,256]{1,0:T(8,128)(2,1)S(1)}, bf16[512,256]{1,0:T(8,128)(2,1)}, u32[]{:S(2)}) copy-start(bf16[512,256]{1,0:T(8,128)(2,1)} %value_ref.3) | copy-start | bytes 786436
  50.4 29.9 %copy-start.5 = (bf16[512,256]{1,0:T(8,128)(2,1)S(1)}, bf16[512,256]{1,0:T(8,128)(2,1)}, u32[]{:S(2)}) copy-start(bf16[512,256]{1,0:T(8,128)(2,1)} %grad_ref.3) | copy-start | bytes 786436
where the time goes:
time: 82.2 us; the launch traced here: 81.8 us
  blocking collectives  67.1 us (82%)
  Pallas kernels  8.94 us (11%)
  local copies, waits for them, and re-layouts  4.92 us (6%)
  between operations  0.83 us (1%)
    all_to_all x2, blocking collectives, exchange(): slabs = lax.all_to_all(slabs, AXES, split_axis=0, concat_axis=0, tiled=True)  67.1 us
    pallas_call x1, Pallas kernels, per_device(): pl.pallas_call(functools.partial(convolve_kernel, groups, per), out_shape...  6.84 us
    unnamed x36, local copies, waits for them, and re-layouts  4.92 us

commit v1 on v0

v1 whole, which is shorter than its diff:
```python
import functools
import math

import jax
import jax.numpy as jnp
import numpy as np
from jax import lax
from jax.experimental import pallas as pl
from jax.experimental.pallas import tpu as pltpu
from jax.sharding import PartitionSpec as P

BLOCK_AXES = ("outer", "inner")
ALL_AXES = ("dp",) + BLOCK_AXES
LANES = 128


def split_table(table):
    table = np.asarray(table, np.float32)
    high = table.astype(jnp.bfloat16)
    low = (table - high.astype(np.float32)).astype(jnp.bfloat16)
    return high, low


def tables(groups, width):
    pieces = width // LANES
    n1 = groups * pieces
    length = n1 * LANES
    order = (np.arange(groups)[None, :] * pieces + np.arange(pieces)[:, None]).reshape(-1)
    k1 = np.arange(n1) + 0.25
    turn = (k1[:, None] * order[None, :]) * (2.0 * math.pi / n1)
    outer = np.concatenate([np.cos(turn), -np.sin(turn)], axis=0)
    back_outer = np.concatenate([np.cos(turn.T), -np.sin(turn.T)], axis=1) / length
    twist = k1[:, None] * np.arange(LANES)[None, :] * (2.0 * math.pi / length)
    lane = np.arange(LANES)
    spin = lane[:, None] * lane[None, :] * (2.0 * math.pi / LANES)
    cos, sin = np.cos(spin), np.sin(spin)
    inner = np.block([[cos, -sin], [sin, cos]])
    back_inner = np.block([[cos, sin], [-sin, cos]])
    return (
        split_table(outer),
        split_table(inner),
        split_table(back_outer),
        split_table(back_inner),
        np.cos(twist).astype(np.float32),
        np.sin(twist).astype(np.float32),
    )


def split(value):
    high = value.astype(jnp.bfloat16)
    low = (value - high.astype(jnp.float32)).astype(jnp.bfloat16)
    return high, low


def dot3(left, right):
    dot = functools.partial(jnp.dot, preferred_element_type=jnp.float32)
    return dot(left[0], right[0]) + (dot(left[0], right[1]) + dot(left[1], right[0]))


def pack_kernel(
    parts, devices, key_hbm, value_hbm, grad_hbm, query_hbm, taps_hbm, out_ref, key, value, grad, query, taps, sems
):
    rows, channels = key.shape
    pieces, per = rows // LANES, channels // devices
    taps_pieces = pieces // parts
    slab = per * (2 * pieces + taps_pieces)
    start = lax.axis_index("dp") * (taps_pieces * LANES)

    def copies(piece):
        span = pl.ds(piece * LANES, LANES)
        moves = [
            pltpu.make_async_copy(src.at[span, :], dst.at[span, :], sems.at[n, piece])
            for n, (src, dst) in enumerate(
                ((key_hbm, key), (value_hbm, value), (grad_hbm, grad), (query_hbm, query))
            )
        ]
        if piece < taps_pieces:
            here = pl.ds(pl.multiple_of(start + piece * LANES, LANES), LANES)
            moves.append(pltpu.make_async_copy(taps_hbm.at[here, :], taps.at[span, :], sems.at[4, piece]))
        return moves

    def put(signal, first, count, piece):
        turned = signal.T
        for c in range(per):
            row = first + c * count + piece
            out_ref[pl.ds(row, devices, stride=slab), :] = turned[c * devices : (c + 1) * devices, :]

    moves = [copies(piece) for piece in range(pieces)]
    for group in moves:
        for move in group:
            move.start()
    for piece in range(pieces):
        for move in moves[piece]:
            move.wait()
        span = slice(piece * LANES, (piece + 1) * LANES)
        put(key[span, :].astype(jnp.float32) * value[span, :].astype(jnp.float32), 0, pieces, piece)
        put(grad[span, :].astype(jnp.float32) * query[span, :].astype(jnp.float32), per * pieces, pieces, piece)
        if piece < taps_pieces:
            put(taps[span, :], 2 * per * pieces, taps_pieces, piece)


def unpack_kernel(
    devices, scale, in_ref, key_ref, value_ref, grad_ref, gq_hbm, gk_hbm, gv_hbm, gf_hbm, gq, gk, gv, gf, sems
):
    rows, channels = key_ref.shape
    pieces, per = rows // LANES, channels // devices
    slab = 3 * per * pieces

    def signal(s, piece):
        parts = [
            in_ref[pl.ds((s * per + c) * pieces + piece, devices, stride=slab), :] for c in range(per)
        ]
        return jnp.concatenate(parts, axis=0).T

    moves = []
    for piece in range(pieces):
        span = slice(piece * LANES, (piece + 1) * LANES)
        gq[span, :] = (grad_ref[span, :].astype(jnp.float32) * signal(0, piece)).astype(gq.dtype)
        corr = signal(1, piece)
        gk[span, :] = (corr * value_ref[span, :].astype(jnp.float32)).astype(gk.dtype)
        gv[span, :] = (corr * key_ref[span, :].astype(jnp.float32)).astype(gv.dtype)
        gf[span, :] = signal(2, piece) * scale
        for n, (src, dst) in enumerate(((gq, gq_hbm), (gk, gk_hbm), (gv, gv_hbm), (gf, gf_hbm))):
            here = pl.ds(piece * LANES, LANES)
            moves.append(pltpu.make_async_copy(src.at[here, :], dst.at[here, :], sems.at[n, piece]))
            moves[-1].start()
    for move in moves:
        move.wait()


def convolve_kernel(
    parts, blocks, per, in_ref, outer_hi, outer_lo, inner_hi, inner_lo,
    back_outer_hi, back_outer_lo, back_inner_hi, back_inner_lo, cos_ref, sin_ref, out_ref,
):
    n1 = cos_ref.shape[0]
    pieces = n1 // blocks
    taps_pieces = pieces // parts
    slab_in = per * (2 * pieces + taps_pieces)
    slab_out = 3 * per * pieces
    outer = (outer_hi[...], outer_lo[...])
    inner = (inner_hi[...], inner_lo[...])
    back_outer = (back_outer_hi[...], back_outer_lo[...])
    back_inner = (back_inner_hi[...], back_inner_lo[...])

    def load(row, part):
        return in_ref[pl.ds(part * blocks * slab_in + row, blocks, stride=slab_in), :]

    def load_signal(s, c, part):
        return jnp.concatenate([load((s * per + c) * pieces + piece, part) for piece in range(pieces)], axis=0)

    def load_taps(c):
        first = (2 * pieces * per) + c * taps_pieces
        return jnp.concatenate(
            [load(first + piece % taps_pieces, piece // taps_pieces) for piece in range(pieces)], axis=0
        )

    def forward(signals):
        mixed = dot3(outer, split(jnp.concatenate(signals, axis=1)))
        spectra = []
        for n in range(len(signals)):
            lanes = slice(n * LANES, (n + 1) * LANES)
            re, im = mixed[:n1, lanes], mixed[n1:, lanes]
            cos, sin = cos_ref[...], sin_ref[...]
            turned = jnp.concatenate([re * cos + im * sin, im * cos - re * sin], axis=1)
            done = dot3(split(turned), inner)
            spectra.append((done[:, :LANES], done[:, LANES:]))
        return spectra

    def product(left, right, sign):
        left_re, left_im = left[0], sign * left[1]
        re = left_re * right[0] - left_im * right[1]
        im = left_re * right[1] + left_im * right[0]
        return jnp.concatenate([re, im], axis=1)

    def inverse(s, c, spectra):
        columns = []
        for spectrum in spectra:
            done = dot3(split(spectrum), back_inner)
            re, im = done[:, :LANES], done[:, LANES:]
            cos, sin = cos_ref[...], sin_ref[...]
            columns.append(jnp.concatenate([re * cos - im * sin, re * sin + im * cos], axis=0))
        signals = dot3(back_outer, split(jnp.concatenate(columns, axis=1)))
        for part in range(len(spectra)):
            for piece in range(pieces):
                row = part * blocks * slab_out + (s * per + c) * pieces + piece
                block = signals[piece * blocks : (piece + 1) * blocks, part * LANES : (part + 1) * LANES]
                out_ref[pl.ds(row, blocks, stride=slab_out), :] = block

    taps = forward([load_taps(c) for c in range(per)])
    for c in range(per):
        mixed = forward([load_signal(0, c, part) for part in range(parts)])
        grad = forward([load_signal(1, c, part) for part in range(parts)])
        inverse(0, c, [product(taps[c], m, 1.0) for m in mixed])
        inverse(1, c, [product(taps[c], g, -1.0) for g in grad])
        inverse(2, c, [product(m, g, -1.0) for m, g in zip(mixed, grad)])


def params(size):
    return pltpu.CompilerParams(vmem_limit_bytes=size << 20)


def exchange(slabs, devices):
    slabs = slabs.reshape(devices, -1, 4, LANES)
    slabs = lax.all_to_all(slabs, ALL_AXES, split_axis=0, concat_axis=0, tiled=True)
    return slabs.reshape(-1, LANES)


def per_device(query_gate, key_gate, value_seq, grad_output, filter_taps):
    parts = lax.axis_size("dp")
    blocks = lax.axis_size(BLOCK_AXES)
    devices = parts * blocks
    rows, channels = query_gate.shape
    per = channels // devices
    pieces = rows // LANES
    outer, inner, back_outer, back_inner, cos, sin = tables(blocks, rows)
    in_hbm = pl.BlockSpec(memory_space=pltpu.HBM)
    in_vmem = pl.BlockSpec(memory_space=pltpu.VMEM)
    gate = pltpu.VMEM((rows, channels), jnp.bfloat16)

    packed = pl.pallas_call(
        functools.partial(pack_kernel, parts, devices),
        out_shape=jax.ShapeDtypeStruct((channels * (2 * pieces + pieces // parts), LANES), jnp.float32),
        in_specs=[in_hbm] * 5,
        out_specs=in_vmem,
        scratch_shapes=[gate] * 4
        + [pltpu.VMEM((rows // parts, channels), jnp.float32), pltpu.SemaphoreType.DMA((5, pieces))],
        compiler_params=params(62),
        name="pack",
    )(key_gate, value_seq, grad_output, query_gate, filter_taps)
    received = exchange(packed, devices)
    results = pl.pallas_call(
        functools.partial(convolve_kernel, parts, blocks, per),
        out_shape=jax.ShapeDtypeStruct((3 * channels * pieces, LANES), jnp.float32),
        compiler_params=params(48),
        name="convolve",
    )(received, *outer, *inner, *back_outer, *back_inner, cos, sin)
    returned = exchange(results, devices)
    narrow = jax.ShapeDtypeStruct((rows, channels), jnp.bfloat16)
    wide = jax.ShapeDtypeStruct((rows, channels), jnp.float32)
    return pl.pallas_call(
        functools.partial(unpack_kernel, devices, 1.0 / math.sqrt(blocks * rows)),
        out_shape=(narrow, narrow, narrow, wide),
        in_specs=[in_vmem] * 4,
        out_specs=[in_hbm] * 4,
        scratch_shapes=[gate] * 3
        + [pltpu.VMEM((rows, channels), jnp.float32), pltpu.SemaphoreType.DMA((4, pieces))],
        compiler_params=params(32),
        name="unpack",
    )(returned, key_gate, value_seq, grad_output)


def solution(mesh):
    split_rows = P(ALL_AXES, None)
    return jax.shard_map(
        per_device,
        mesh=mesh,
        in_specs=(split_rows, split_rows, split_rows, split_rows, P(BLOCK_AXES, None)),
        out_specs=(split_rows, split_rows, split_rows, split_rows),
        check_vma=False,
    )
```

time: 82.2 us -> 73.8 us (0.90)
  local copies, waits for them, and re-layouts: 4.92 us -> 0.09 us
  blocking collectives: 67.1 us -> 62.4 us
  Pallas kernels: 8.94 us -> 10.3 us
    unnamed x36 -> x26, local copies, waits for them, and re-layouts: 4.92 us -> 0.09 us
    all_to_all x2, blocking collectives: 67.1 us -> 62.4 us  [exchange(): lax.all_to_all(slabs, ALL_AXES, split_axis=0, concat_axis=0, tiled=True)]
    pallas_call x3, Pallas kernels: 8.94 us -> 10.3 us  [the longest x1 6.07 us: per_device(): pl.pallas_call(functools.partial(convolve_kernel, parts, blocks, per), ou...]
where the time goes in v1:
time: 73.8 us; the launch traced here: 73.6 us
  blocking collectives  62.4 us (85%)
  Pallas kernels  10.3 us (14%)
  between operations  0.81 us (1%)
    all_to_all x2, blocking collectives, exchange(): lax.all_to_all(slabs, ALL_AXES, split_axis=0, concat_axis=0, tiled=True)  62.4 us
    pallas_call x1, Pallas kernels, per_device(): pl.pallas_call(functools.partial(convolve_kernel, parts, blocks, per), ou...  6.07 us
    pallas_call x1, Pallas kernels, per_device(): pl.pallas_call(functools.partial(pack_kernel, parts, devices), out_shape=...  2.94 us

profile of v1, /device:TPU:1, one launch (start us, length us, event | category | flops | bytes accessed | tf_op | source)
XLA Modules:
  0.0 73.6 jit_solution(12519543522302991370)
XLA Ops:
  0.6 2.9 %pack.1 = f32[2560,128]{1,0:T(8,128)} custom-call(bf16[512,256]{1,0:T(8,128)(2,1)} %key_ref.1, bf16[512,256]{1,0:T(8,128)(2,1)} %value_ref.1, bf16[512,256]{1,0:T(8,128)(2,1)} %grad_ref.1, bf16[512,256]{1,0:T(8,128)(2,1)} %query_hbm.1, f32[512,256]{1,0:T(8,128)} %taps_hbm.1), custom_call_target="tpu_custom_call" | custom-call | tf_op jit(solution)/shard_map/pack/pallas_call | solution.py:220
  3.6 0.0 copy-start.3
  3.6 0.0 copy-start.4
  3.6 0.0 copy-start.5
  3.6 0.0 copy-start.6
  3.6 0.0 copy-start.7
  3.6 0.0 copy-start.8
  3.7 0.0 copy-start.9
  3.7 0.0 copy-start.10
  3.7 0.0 copy-start.11
  3.7 0.0 copy-start.12
  3.7 33.4 %all_to_all.10 = f32[128,5,4,128]{3,2,1,0:T(4,128)S(1)} all-to-all(f32[128,5,4,128]{3,2,1,0:T(4,128)} %bitcast.7), channel_id=1, replica_groups=mesh['dp'=2,'outer'=4,'inner'=16] {'dp','outer','inner'}, dimensions={0} | all-to-all | bytes 2621440 | tf_op jit(solution)/shard_map/all_to_all | solution.py:204
  37.1 0.0 copy-done.3
  37.1 0.0 copy-done.4
  37.1 0.0 copy-done.5
  37.1 0.0 copy-done.6
  37.1 0.0 copy-done.7
  37.2 6.1 %convolve.1 = f32[3072,128]{1,0:T(8,128)S(1)} custom-call(f32[2560,128]{1,0:T(8,128)S(1)} %bitcast.6, bf16[512,256]{1,0:T(8,128)(2,1)S(1)} %copy-done.6, bf16[512,256]{1,0:T(8,128)(2,1)S(1)} %copy-done.5, bf16[256,256]{1,0:T(8,128)(2,1)S(1)} %copy-done.12, bf16[256,256]{1,0:T(8,128)(2,1)S(1)} %copy-done.11, bf16[256,512]{1,0:T(8,128)(2,1)S(1)} %copy-done.4, ...), custom_call_target="tpu_custom_call" | custom-call | tf_op jit(solution)/shard_map/convolve/pallas_call | solution.py:231
  43.2 0.0 copy-start
  43.3 0.0 copy-start.1
  43.3 0.0 copy-start.2
  43.3 29.0 %all_to_all.11 = f32[128,6,4,128]{3,2,1,0:T(4,128)S(1)} all-to-all(f32[128,6,4,128]{3,2,1,0:T(4,128)S(1)} %bitcast.5), channel_id=1, replica_groups=mesh['dp'=2,'outer'=4,'inner'=16] {'dp','outer','inner'}, dimensions={0} | all-to-all | bytes 3145728 | tf_op jit(solution)/shard_map/all_to_all | solution.py:204
  72.3 0.0 copy-done.2
  72.3 1.3 %unpack.1 = (bf16[512,256]{1,0:T(8,128)(2,1)}, bf16[512,256]{1,0:T(8,128)(2,1)}, bf16[512,256]{1,0:T(8,128)(2,1)}, f32[512,256]{1,0:T(8,128)}) custom-call(f32[3072,128]{1,0:T(8,128)S(1)} %bitcast.4, bf16[512,256]{1,0:T(8,128)(2,1)S(1)} %copy-done, bf16[512,256]{1,0:T(8,128)(2,1)S(1)} %copy-done.1, bf16[512,256]{1,0:T(8,128)(2,1)S(1)} %copy-done.2), custom_call_target="tpu_custom_call" | custom-call | tf_op jit(solution)/shard_map/unpack/pallas_call | solution.py:240
  (7 shorter events, 0.0 us)
Async XLA Ops:
  3.6 33.5 %copy-start.3 = (bf16[256,512]{1,0:T(8,128)(2,1)S(1)}, bf16[256,512]{1,0:T(8,128)(2,1)}, u32[]{:S(2)}) copy-start(bf16[256,512]{1,0:T(8,128)(2,1)} %constant.25.clone.back_outer_lo) | copy-start | bytes 786436
  3.6 33.5 %copy-start.4 = (bf16[256,512]{1,0:T(8,128)(2,1)S(1)}, bf16[256,512]{1,0:T(8,128)(2,1)}, u32[]{:S(2)}) copy-start(bf16[256,512]{1,0:T(8,128)(2,1)} %constant.24.clone.back_outer_hi) | copy-start | bytes 786436
  3.6 33.5 %copy-start.5 = (bf16[512,256]{1,0:T(8,128)(2,1)S(1)}, bf16[512,256]{1,0:T(8,128)(2,1)}, u32[]{:S(2)}) copy-start(bf16[512,256]{1,0:T(8,128)(2,1)} %constant.21.clone.outer_lo) | copy-start | bytes 786436
  3.6 33.5 %copy-start.6 = (bf16[512,256]{1,0:T(8,128)(2,1)S(1)}, bf16[512,256]{1,0:T(8,128)(2,1)}, u32[]{:S(2)}) copy-start(bf16[512,256]{1,0:T(8,128)(2,1)} %constant.20.clone.outer_hi) | copy-start | bytes 786436
  3.6 33.5 %copy-start.7 = (f32[256,128]{1,0:T(8,128)S(1)}, f32[256,128]{1,0:T(8,128)}, u32[]{:S(2)}) copy-start(f32[256,128]{1,0:T(8,128)} %constant.29.clone.sin_ref) | copy-start | bytes 393220
  3.6 33.5 %copy-start.8 = (f32[256,128]{1,0:T(8,128)S(1)}, f32[256,128]{1,0:T(8,128)}, u32[]{:S(2)}) copy-start(f32[256,128]{1,0:T(8,128)} %constant.28.clone.cos_ref) | copy-start | bytes 393220
  3.7 33.5 %copy-start.9 = (bf16[256,256]{1,0:T(8,128)(2,1)S(1)}, bf16[256,256]{1,0:T(8,128)(2,1)}, u32[]{:S(2)}) copy-start(bf16[256,256]{1,0:T(8,128)(2,1)} %constant.27.clone.back_inner_lo) | copy-start | bytes 393220
  3.7 33.5 %copy-start.10 = (bf16[256,256]{1,0:T(8,128)(2,1)S(1)}, bf16[256,256]{1,0:T(8,128)(2,1)}, u32[]{:S(2)}) copy-start(bf16[256,256]{1,0:T(8,128)(2,1)} %constant.26.clone.back_inner_hi) | copy-start | bytes 393220
  3.7 33.5 %copy-start.11 = (bf16[256,256]{1,0:T(8,128)(2,1)S(1)}, bf16[256,256]{1,0:T(8,128)(2,1)}, u32[]{:S(2)}) copy-start(bf16[256,256]{1,0:T(8,128)(2,1)} %constant.23.clone.inner_lo) | copy-start | bytes 393220
  3.7 33.5 %copy-start.12 = (bf16[256,256]{1,0:T(8,128)(2,1)S(1)}, bf16[256,256]{1,0:T(8,128)(2,1)}, u32[]{:S(2)}) copy-start(bf16[256,256]{1,0:T(8,128)(2,1)} %constant.22.clone.inner_hi) | copy-start | bytes 393220
  43.2 29.0 %copy-start = (bf16[512,256]{1,0:T(8,128)(2,1)S(1)}, bf16[512,256]{1,0:T(8,128)(2,1)}, u32[]{:S(2)}) copy-start(bf16[512,256]{1,0:T(8,128)(2,1)} %key_ref.1) | copy-start | bytes 786436
  43.3 29.0 %copy-start.1 = (bf16[512,256]{1,0:T(8,128)(2,1)S(1)}, bf16[512,256]{1,0:T(8,128)(2,1)}, u32[]{:S(2)}) copy-start(bf16[512,256]{1,0:T(8,128)(2,1)} %value_ref.1) | copy-start | bytes 786436
  43.3 29.0 %copy-start.2 = (bf16[512,256]{1,0:T(8,128)(2,1)S(1)}, bf16[512,256]{1,0:T(8,128)(2,1)}, u32[]{:S(2)}) copy-start(bf16[512,256]{1,0:T(8,128)(2,1)} %grad_ref.1) | copy-start | bytes 786436

commit v2 on v1

--- a/solution.py
+++ b/solution.py
@@ -154,45 +154,72 @@
             [load(first + piece % taps_pieces, piece // taps_pieces) for piece in range(pieces)], axis=0
         )
 
-    def forward(signals):
+    def outer_step(signals):
         mixed = dot3(outer, split(jnp.concatenate(signals, axis=1)))
-        spectra = []
+        turned = []
         for n in range(len(signals)):
             lanes = slice(n * LANES, (n + 1) * LANES)
             re, im = mixed[:n1, lanes], mixed[n1:, lanes]
             cos, sin = cos_ref[...], sin_ref[...]
-            turned = jnp.concatenate([re * cos + im * sin, im * cos - re * sin], axis=1)
-            done = dot3(split(turned), inner)
-            spectra.append((done[:, :LANES], done[:, LANES:]))
-        return spectra
+            turned.append(jnp.concatenate([re * cos + im * sin, im * cos - re * sin], axis=1))
+        return split(jnp.concatenate(turned, axis=0))
+
+    def inner_step(turned):
+        return dot3(turned, inner)
 
     def product(left, right, sign):
-        left_re, left_im = left[0], sign * left[1]
-        re = left_re * right[0] - left_im * right[1]
-        im = left_re * right[1] + left_im * right[0]
+        left_re, left_im = left[:, :LANES], sign * left[:, LANES:]
+        right_re, right_im = right[:, :LANES], right[:, LANES:]
+        re = left_re * right_re - left_im * right_im
+        im = left_re * right_im + left_im * right_re
         return jnp.concatenate([re, im], axis=1)
 
-    def inverse(s, c, spectra):
+    def back_inner_step(products):
+        done = dot3(split(products), back_inner)
         columns = []
-        for spectrum in spectra:
-            done = dot3(split(spectrum), back_inner)
-            re, im = done[:, :LANES], done[:, LANES:]
+        for n in range(parts):
+            re, im = done[n * n1 : (n + 1) * n1, :LANES], done[n * n1 : (n + 1) * n1, LANES:]
             cos, sin = cos_ref[...], sin_ref[...]
             columns.append(jnp.concatenate([re * cos - im * sin, re * sin + im * cos], axis=0))
-        signals = dot3(back_outer, split(jnp.concatenate(columns, axis=1)))
-        for part in range(len(spectra)):
+        return jnp.concatenate(columns, axis=1)
+
+    def back_outer_step(s, c, columns):
+        signals = dot3(back_outer, split(columns))
+        for part in range(parts):
             for piece in range(pieces):
                 row = part * blocks * slab_out + (s * per + c) * pieces + piece
                 block = signals[piece * blocks : (piece + 1) * blocks, part * LANES : (part + 1) * LANES]
                 out_ref[pl.ds(row, blocks, stride=slab_out), :] = block
 
-    taps = forward([load_taps(c) for c in range(per)])
-    for c in range(per):
-        mixed = forward([load_signal(0, c, part) for part in range(parts)])
-        grad = forward([load_signal(1, c, part) for part in range(parts)])
-        inverse(0, c, [product(taps[c], m, 1.0) for m in mixed])
-        inverse(1, c, [product(taps[c], g, -1.0) for g in grad])
-        inverse(2, c, [product(m, g, -1.0) for m, g in zip(mixed, grad)])
+    def signal(s, c):
+        return [load_signal(s, c, part) for part in range(parts)]
+
+    def many(one):
+        return jnp.concatenate([one] * parts, axis=0)
+
+    t = outer_step([load_taps(c) for c in range(per)])
+    m0 = outer_step(signal(0, 0))
+    t = inner_step(t)
+    taps = [many(t[c * n1 : (c + 1) * n1]) for c in range(per)]
+    g0 = outer_step(signal(1, 0))
+    m0 = inner_step(m0)
+    m1 = outer_step(signal(0, 1))
+    conv0 = back_inner_step(product(taps[0], m0, 1.0))
+    g0 = inner_step(g0)
+    g1 = outer_step(signal(1, 1))
+    back_outer_step(0, 0, conv0)
+    corr0 = back_inner_step(product(taps[0], g0, -1.0))
+    m1 = inner_step(m1)
+    back_outer_step(1, 0, corr0)
+    cross0 = back_inner_step(product(m0, g0, -1.0))
+    g1 = inner_step(g1)
+    back_outer_step(2, 0, cross0)
+    conv1 = back_inner_step(product(taps[1], m1, 1.0))
+    corr1 = back_inner_step(product(taps[1], g1, -1.0))
+    back_outer_step(0, 1, conv1)
+    cross1 = back_inner_step(product(m1, g1, -1.0))
+    back_outer_step(1, 1, corr1)
+    back_outer_step(2, 1, cross1)
 
 
 def params(size):
@@ -224,9 +251,9 @@
         out_specs=in_vmem,
         scratch_shapes=[gate] * 4
         + [pltpu.VMEM((rows // parts, channels), jnp.float32), pltpu.SemaphoreType.DMA((5, pieces))],
-        compiler_params=params(62),
+        compiler_params=params(32),
         name="pack",
-    )(key_gate, value_seq, grad_output, query_gate, filter_taps)
+    )(*(pltpu.with_memory_space_constraint(x, pltpu.HBM) for x in (key_gate, value_seq, grad_output, query_gate, filter_taps)))
     received = exchange(packed, devices)
     results = pl.pallas_call(
         functools.partial(convolve_kernel, parts, blocks, per),

time: 73.8 us -> 71.8 us (0.973)
  Pallas kernels: 10.3 us -> 8.58 us
    pallas_call x1, Pallas kernels: 2.94 us -> 1.85 us  [per_device(): pl.pallas_call(functools.partial(pack_kernel, parts, devices), out_shape=...]
where the time goes in v2:
time: 71.8 us; the launch traced here: 71.6 us
  blocking collectives  62.2 us (87%)
  Pallas kernels  8.58 us (12%)
  between operations  0.81 us (1%)
    all_to_all x2, blocking collectives, exchange(): lax.all_to_all(slabs, ALL_AXES, split_axis=0, concat_axis=0, tiled=True)  62.2 us
    pallas_call x1, Pallas kernels, per_device(): pl.pallas_call(functools.partial(convolve_kernel, parts, blocks, per), ou...  5.43 us
    pallas_call x1, Pallas kernels, per_device(): pl.pallas_call(functools.partial(pack_kernel, parts, devices), out_shape=...  1.85 us

profile of v2, /device:TPU:1, one launch (start us, length us, event | category | flops | bytes accessed | tf_op | source)
XLA Modules:
  0.0 71.6 jit_solution(9977310455167659776)
XLA Ops:
  0.6 1.9 %pack.1 = f32[2560,128]{1,0:T(8,128)S(1)} custom-call(bf16[512,256]{1,0:T(8,128)(2,1)} %key_ref.1, bf16[512,256]{1,0:T(8,128)(2,1)} %value_ref.1, bf16[512,256]{1,0:T(8,128)(2,1)} %grad_ref.1, bf16[512,256]{1,0:T(8,128)(2,1)} %query_hbm.1, f32[512,256]{1,0:T(8,128)} %taps_hbm.1), custom_call_target="tpu_custom_call" | custom-call | tf_op jit(solution)/shard_map/pack/pallas_call | solution.py:247
  2.5 0.0 copy-start.3
  2.5 0.0 copy-start.4
  2.5 0.0 copy-start.5
  2.5 0.0 copy-start.6
  2.5 0.0 copy-start.7
  2.6 0.0 copy-start.8
  2.6 0.0 copy-start.9
  2.6 0.0 copy-start.10
  2.6 0.0 copy-start.11
  2.6 0.0 copy-start.12
  2.6 33.2 %all_to_all.10 = f32[128,5,4,128]{3,2,1,0:T(4,128)S(1)} all-to-all(f32[128,5,4,128]{3,2,1,0:T(4,128)S(1)} %bitcast.7), channel_id=1, replica_groups=mesh['dp'=2,'outer'=4,'inner'=16] {'dp','outer','inner'}, dimensions={0} | all-to-all | bytes 2621440 | tf_op jit(solution)/shard_map/all_to_all | solution.py:231
  35.8 0.0 copy-done.3
  35.8 0.0 copy-done.4
  35.8 0.0 copy-done.5
  35.8 0.0 copy-done.6
  35.8 0.0 copy-done.7
  35.9 5.4 %convolve.1 = f32[3072,128]{1,0:T(8,128)S(1)} custom-call(f32[2560,128]{1,0:T(8,128)S(1)} %bitcast.6, bf16[512,256]{1,0:T(8,128)(2,1)S(1)} %copy-done.6, bf16[512,256]{1,0:T(8,128)(2,1)S(1)} %copy-done.5, bf16[256,256]{1,0:T(8,128)(2,1)S(1)} %copy-done.12, bf16[256,256]{1,0:T(8,128)(2,1)S(1)} %copy-done.11, bf16[256,512]{1,0:T(8,128)(2,1)S(1)} %copy-done.4, ...), custom_call_target="tpu_custom_call" | custom-call | tf_op jit(solution)/shard_map/convolve/pallas_call | solution.py:258
  41.3 0.0 copy-start
  41.3 0.0 copy-start.1
  41.3 0.0 copy-start.2
  41.3 29.0 %all_to_all.11 = f32[128,6,4,128]{3,2,1,0:T(4,128)S(1)} all-to-all(f32[128,6,4,128]{3,2,1,0:T(4,128)S(1)} %bitcast.5), channel_id=1, replica_groups=mesh['dp'=2,'outer'=4,'inner'=16] {'dp','outer','inner'}, dimensions={0} | all-to-all | bytes 3145728 | tf_op jit(solution)/shard_map/all_to_all | solution.py:231
  70.3 0.0 copy-done.1
  70.3 1.3 %unpack.1 = (bf16[512,256]{1,0:T(8,128)(2,1)}, bf16[512,256]{1,0:T(8,128)(2,1)}, bf16[512,256]{1,0:T(8,128)(2,1)}, f32[512,256]{1,0:T(8,128)}) custom-call(f32[3072,128]{1,0:T(8,128)S(1)} %bitcast.4, bf16[512,256]{1,0:T(8,128)(2,1)S(1)} %copy-done, bf16[512,256]{1,0:T(8,128)(2,1)S(1)} %copy-done.1, bf16[512,256]{1,0:T(8,128)(2,1)S(1)} %copy-done.2), custom_call_target="tpu_custom_call" | custom-call | tf_op jit(solution)/shard_map/unpack/pallas_call | solution.py:267
  (7 shorter events, 0.0 us)
Async XLA Ops:
  2.5 33.3 %copy-start.3 = (bf16[256,512]{1,0:T(8,128)(2,1)S(1)}, bf16[256,512]{1,0:T(8,128)(2,1)}, u32[]{:S(2)}) copy-start(bf16[256,512]{1,0:T(8,128)(2,1)} %constant.25.clone.back_outer_lo) | copy-start | bytes 786436
  2.5 33.3 %copy-start.4 = (bf16[256,512]{1,0:T(8,128)(2,1)S(1)}, bf16[256,512]{1,0:T(8,128)(2,1)}, u32[]{:S(2)}) copy-start(bf16[256,512]{1,0:T(8,128)(2,1)} %constant.24.clone.back_outer_hi) | copy-start | bytes 786436
  2.5 33.3 %copy-start.5 = (bf16[512,256]{1,0:T(8,128)(2,1)S(1)}, bf16[512,256]{1,0:T(8,128)(2,1)}, u32[]{:S(2)}) copy-start(bf16[512,256]{1,0:T(8,128)(2,1)} %constant.21.clone.outer_lo) | copy-start | bytes 786436
  2.5 33.3 %copy-start.6 = (bf16[512,256]{1,0:T(8,128)(2,1)S(1)}, bf16[512,256]{1,0:T(8,128)(2,1)}, u32[]{:S(2)}) copy-start(bf16[512,256]{1,0:T(8,128)(2,1)} %constant.20.clone.outer_hi) | copy-start | bytes 786436
  2.5 33.3 %copy-start.7 = (f32[256,128]{1,0:T(8,128)S(1)}, f32[256,128]{1,0:T(8,128)}, u32[]{:S(2)}) copy-start(f32[256,128]{1,0:T(8,128)} %constant.29.clone.sin_ref) | copy-start | bytes 393220
  2.6 33.3 %copy-start.8 = (f32[256,128]{1,0:T(8,128)S(1)}, f32[256,128]{1,0:T(8,128)}, u32[]{:S(2)}) copy-start(f32[256,128]{1,0:T(8,128)} %constant.28.clone.cos_ref) | copy-start | bytes 393220
  2.6 33.3 %copy-start.9 = (bf16[256,256]{1,0:T(8,128)(2,1)S(1)}, bf16[256,256]{1,0:T(8,128)(2,1)}, u32[]{:S(2)}) copy-start(bf16[256,256]{1,0:T(8,128)(2,1)} %constant.27.clone.back_inner_lo) | copy-start | bytes 393220
  2.6 33.3 %copy-start.10 = (bf16[256,256]{1,0:T(8,128)(2,1)S(1)}, bf16[256,256]{1,0:T(8,128)(2,1)}, u32[]{:S(2)}) copy-start(bf16[256,256]{1,0:T(8,128)(2,1)} %constant.26.clone.back_inner_hi) | copy-start | bytes 393220
  2.6 33.3 %copy-start.11 = (bf16[256,256]{1,0:T(8,128)(2,1)S(1)}, bf16[256,256]{1,0:T(8,128)(2,1)}, u32[]{:S(2)}) copy-start(bf16[256,256]{1,0:T(8,128)(2,1)} %constant.23.clone.inner_lo) | copy-start | bytes 393220
  2.6 33.2 %copy-start.12 = (bf16[256,256]{1,0:T(8,128)(2,1)S(1)}, bf16[256,256]{1,0:T(8,128)(2,1)}, u32[]{:S(2)}) copy-start(bf16[256,256]{1,0:T(8,128)(2,1)} %constant.22.clone.inner_hi) | copy-start | bytes 393220
  41.3 29.0 %copy-start = (bf16[512,256]{1,0:T(8,128)(2,1)S(1)}, bf16[512,256]{1,0:T(8,128)(2,1)}, u32[]{:S(2)}) copy-start(bf16[512,256]{1,0:T(8,128)(2,1)} %key_ref.1) | copy-start | bytes 786436
  41.3 29.0 %copy-start.1 = (bf16[512,256]{1,0:T(8,128)(2,1)S(1)}, bf16[512,256]{1,0:T(8,128)(2,1)}, u32[]{:S(2)}) copy-start(bf16[512,256]{1,0:T(8,128)(2,1)} %value_ref.1) | copy-start | bytes 786436
  41.3 29.0 %copy-start.2 = (bf16[512,256]{1,0:T(8,128)(2,1)S(1)}, bf16[512,256]{1,0:T(8,128)(2,1)}, u32[]{:S(2)}) copy-start(bf16[512,256]{1,0:T(8,128)(2,1)} %grad_ref.1) | copy-start | bytes 786436

commit v3 on v2

v3 whole, which is shorter than its diff:
```python
import functools
import math

import jax
import jax.numpy as jnp
import numpy as np
from jax import lax
from jax.experimental import pallas as pl
from jax.experimental.pallas import tpu as pltpu
from jax.sharding import PartitionSpec as P

BLOCK_AXES = ("outer", "inner")
ALL_AXES = ("dp",) + BLOCK_AXES
LANES = 128


def split_table(table):
    table = np.asarray(table, np.float32)
    high = table.astype(jnp.bfloat16)
    low = (table - high.astype(np.float32)).astype(jnp.bfloat16)
    return high, low


def square_table(table):
    high, low = split_table(table)
    return np.block([[high, low], [high, np.zeros_like(low)]])


def tables(groups, width):
    pieces = width // LANES
    n1 = groups * pieces
    length = n1 * LANES
    order = (np.arange(groups)[None, :] * pieces + np.arange(pieces)[:, None]).reshape(-1)
    k1 = np.arange(n1) + 0.25
    turn = (k1[:, None] * order[None, :]) * (2.0 * math.pi / n1)
    outer = np.concatenate([np.cos(turn), -np.sin(turn)], axis=0)
    back_outer = np.concatenate([np.cos(turn.T), -np.sin(turn.T)], axis=1) / length
    twist = k1[:, None] * np.arange(LANES)[None, :] * (2.0 * math.pi / length)
    half = np.arange(LANES // 2)
    even = half[:, None] * half[None, :] * (4.0 * math.pi / LANES)
    odd = half[:, None] * (2 * half[None, :] + 1) * (2.0 * math.pi / LANES)
    inner_even = np.block([[np.cos(even), -np.sin(even)], [np.sin(even), np.cos(even)]])
    inner_odd = np.block([[np.cos(odd), -np.sin(odd)], [-np.sin(odd), -np.cos(odd)]])
    back_even = np.block([[np.cos(even.T), np.sin(even.T)], [-np.sin(even.T), np.cos(even.T)]])
    back_odd = np.block([[np.cos(odd.T), np.sin(odd.T)], [-np.sin(odd.T), np.cos(odd.T)]])
    back_high, back_low = split_table(back_outer)
    narrow = [
        *split_table(outer),
        *(half for whole in (back_high, back_low) for half in np.split(whole, 2, axis=1)),
        *(square_table(t) for t in (inner_even, inner_odd, back_even, back_odd)),
    ]
    return np.concatenate(narrow, axis=0), np.stack([np.cos(twist), np.sin(twist)]).astype(np.float32)


def split(value):
    high = value.astype(jnp.bfloat16)
    low = (value - high.astype(jnp.float32)).astype(jnp.bfloat16)
    return high, low


def dot3(left, right):
    wide = jnp.concatenate([left[0], left[1], left[0]], axis=1)
    tall = jnp.concatenate([right[0], right[0], right[1]], axis=0)
    return jnp.dot(wide, tall, preferred_element_type=jnp.float32)


def dot_square(value, table):
    sums = jnp.dot(jnp.concatenate(split(value), axis=1), table, preferred_element_type=jnp.float32)
    return sums[:, :LANES] + sums[:, LANES:]


def pack_kernel(
    parts, devices, key_hbm, value_hbm, grad_hbm, query_hbm, taps_hbm, out_ref, key, value, grad, query, taps, sems
):
    rows, channels = key.shape
    pieces, per = rows // LANES, channels // devices
    taps_rows = rows // parts
    taps_pieces = taps_rows // LANES
    slab = per * (2 * pieces + taps_pieces)
    start = pl.multiple_of(lax.axis_index("dp") * taps_rows, taps_rows)

    def put(signal, first, count, piece):
        turned = signal.T
        for c in range(per):
            row = first + c * count + piece
            out_ref[pl.ds(row, devices, stride=slab), :] = turned[c * devices : (c + 1) * devices, :]

    def put_product(left, right, first):
        for piece in range(pieces):
            span = slice(piece * LANES, (piece + 1) * LANES)
            put(left[span, :].astype(jnp.float32) * right[span, :].astype(jnp.float32), first, pieces, piece)

    sources = (key_hbm, value_hbm, taps_hbm.at[pl.ds(start, taps_rows), :], grad_hbm, query_hbm)
    targets = (key, value, taps, grad, query)
    moves = [pltpu.make_async_copy(src, dst, sems.at[n]) for n, (src, dst) in enumerate(zip(sources, targets))]
    for move in moves:
        move.start()
    moves[0].wait()
    moves[1].wait()
    put_product(key, value, 0)
    moves[2].wait()
    for piece in range(taps_pieces):
        put(taps[piece * LANES : (piece + 1) * LANES, :], 2 * per * pieces, taps_pieces, piece)
    moves[3].wait()
    moves[4].wait()
    put_product(grad, query, per * pieces)


def unpack_kernel(
    devices, scale, in_ref, key_ref, value_ref, grad_ref, gq_hbm, gk_hbm, gv_hbm, gf_hbm, gq, gk, gv, gf, sems
):
    rows, channels = key_ref.shape
    pieces, per = rows // LANES, channels // devices
    slab = 3 * per * pieces

    def signal(s, piece):
        parts = [
            in_ref[pl.ds((s * per + c) * pieces + piece, devices, stride=slab), :] for c in range(per)
        ]
        return jnp.concatenate(parts, axis=0).T

    moves = []
    for piece in range(pieces):
        span = slice(piece * LANES, (piece + 1) * LANES)
        gq[span, :] = (grad_ref[span, :].astype(jnp.float32) * signal(0, piece)).astype(gq.dtype)
        corr = signal(1, piece)
        gk[span, :] = (corr * value_ref[span, :].astype(jnp.float32)).astype(gk.dtype)
        gv[span, :] = (corr * key_ref[span, :].astype(jnp.float32)).astype(gv.dtype)
        gf[span, :] = signal(2, piece) * scale
        for n, (src, dst) in enumerate(((gq, gq_hbm), (gk, gk_hbm), (gv, gv_hbm), (gf, gf_hbm))):
            here = pl.ds(piece * LANES, LANES)
            moves.append(pltpu.make_async_copy(src.at[here, :], dst.at[here, :], sems.at[n, piece]))
            moves[-1].start()
    for move in moves:
        move.wait()


def convolve_kernel(parts, blocks, per, in_ref, tables_ref, twist_ref, out_ref):
    n1 = twist_ref.shape[1]
    pieces = n1 // blocks
    taps_pieces = pieces // parts
    slab_in = per * (2 * pieces + taps_pieces)
    slab_out = 3 * per * pieces
    square = 2 * LANES

    def table(start, rows):
        return tables_ref[start : start + rows, :]

    def wide_table(start):
        return jnp.concatenate([table(start, n1), table(start + n1, n1)], axis=1)

    outer = (table(0, 2 * n1), table(2 * n1, 2 * n1))
    back_outer = (wide_table(4 * n1), wide_table(6 * n1))
    even, odd, back_even, back_odd = (table(8 * n1 + n * square, square) for n in range(4))

    def first_half(left, right):
        lane = lax.broadcasted_iota(jnp.int32, left.shape, 1)
        return jnp.where(lane < LANES // 2, left, right)

    def swap(value):
        return pltpu.roll(value, LANES // 2, 1)

    def load(row, part):
        return in_ref[pl.ds(part * blocks * slab_in + row, blocks, stride=slab_in), :]

    def load_signal(s, c, part):
        return jnp.concatenate([load((s * per + c) * pieces + piece, part) for piece in range(pieces)], axis=0)

    def load_taps(c):
        first = (2 * pieces * per) + c * taps_pieces
        return jnp.concatenate(
            [load(first + piece % taps_pieces, piece // taps_pieces) for piece in range(pieces)], axis=0
        )

    def outer_step(signals):
        mixed = dot3(outer, split(jnp.concatenate(signals, axis=1)))
        ups, downs = [], []
        for n in range(len(signals)):
            lanes = slice(n * LANES, (n + 1) * LANES)
            re, im = mixed[:n1, lanes], mixed[n1:, lanes]
            cos, sin = twist_ref[0], twist_ref[1]
            re, im = re * cos + im * sin, im * cos - re * sin
            near, far = first_half(re, im), swap(first_half(im, re))
            ups.append(near + far)
            downs.append(near - far)
        return jnp.concatenate(ups, axis=0), jnp.concatenate(downs, axis=0)

    def inner_step(turned):
        spectra = (dot_square(turned[0], even), dot_square(turned[1], odd))
        return [(one, swap(one)) for one in spectra]

    def factors(spectra):
        return [(first_half(one, other), first_half(-other, one)) for one, other in spectra]

    def product(left, right):
        return [one * re + other * im for (one, other), (re, im) in zip(left, right)]

    def product_conjugate(left, right):
        return [one * re - other * im for (one, other), (re, im) in zip(left, right)]

    def back_inner_step(products):
        sums_even, sums_odd = dot_square(products[0], back_even), dot_square(products[1], back_odd)
        near, far = sums_even + sums_odd, sums_even - sums_odd
        turned = swap(first_half(far, near))
        res, ims = first_half(near, turned), first_half(turned, far)
        columns = []
        for n in range(parts):
            re, im = res[n * n1 : (n + 1) * n1], ims[n * n1 : (n + 1) * n1]
            cos, sin = twist_ref[0], twist_ref[1]
            columns.append(jnp.concatenate([re * cos - im * sin, re * sin + im * cos], axis=0))
        return jnp.concatenate(columns, axis=1)

    def back_outer_step(s, c, columns):
        signals = dot3(back_outer, split(columns))
        for part in range(parts):
            for piece in range(pieces):
                row = part * blocks * slab_out + (s * per + c) * pieces + piece
                block = signals[piece * blocks : (piece + 1) * blocks, part * LANES : (part + 1) * LANES]
                out_ref[pl.ds(row, blocks, stride=slab_out), :] = block

    def signal(s, c):
        return [load_signal(s, c, part) for part in range(parts)]

    def channel(pair, c):
        one = pair[c * n1 : (c + 1) * n1]
        return jnp.concatenate([one] * parts, axis=0)

    m0 = outer_step(signal(0, 0))
    g0 = outer_step(signal(1, 0))
    t = outer_step([load_taps(c) for c in range(per)])
    m0 = inner_step(m0)
    g0 = inner_step(g0)
    t = factors(inner_step(t))
    taps = [[tuple(channel(f, c) for f in half) for half in t] for c in range(per)]
    m1 = outer_step(signal(0, 1))
    g1 = outer_step(signal(1, 1))
    cross0 = back_inner_step(product_conjugate(g0, factors(m0)))
    conv0 = back_inner_step(product(m0, taps[0]))
    corr0 = back_inner_step(product_conjugate(g0, taps[0]))
    back_outer_step(2, 0, cross0)
    back_outer_step(0, 0, conv0)
    back_outer_step(1, 0, corr0)
    m1 = inner_step(m1)
    g1 = inner_step(g1)
    cross1 = back_inner_step(product_conjugate(g1, factors(m1)))
    conv1 = back_inner_step(product(m1, taps[1]))
    corr1 = back_inner_step(product_conjugate(g1, taps[1]))
    back_outer_step(2, 1, cross1)
    back_outer_step(0, 1, conv1)
    back_outer_step(1, 1, corr1)


def params(size):
    return pltpu.CompilerParams(vmem_limit_bytes=size << 20)


def exchange(slabs, devices):
    slabs = slabs.reshape(devices, -1, 4, LANES)
    slabs = lax.all_to_all(slabs, ALL_AXES, split_axis=0, concat_axis=0, tiled=True)
    return slabs.reshape(-1, LANES)


def per_device(query_gate, key_gate, value_seq, grad_output, filter_taps):
    parts = lax.axis_size("dp")
    blocks = lax.axis_size(BLOCK_AXES)
    devices = parts * blocks
    rows, channels = query_gate.shape
    per = channels // devices
    pieces = rows // LANES
    operands = (key_gate, value_seq, grad_output, query_gate, filter_taps)
    in_hbm = pl.BlockSpec(memory_space=pltpu.HBM)
    in_vmem = pl.BlockSpec(memory_space=pltpu.VMEM)
    gate = pltpu.VMEM((rows, channels), jnp.bfloat16)

    packed = pl.pallas_call(
        functools.partial(pack_kernel, parts, devices),
        out_shape=jax.ShapeDtypeStruct((channels * (2 * pieces + pieces // parts), LANES), jnp.float32),
        in_specs=[in_hbm] * 5,
        out_specs=in_vmem,
        scratch_shapes=[gate] * 4
        + [pltpu.VMEM((rows // parts, channels), jnp.float32), pltpu.SemaphoreType.DMA((5,))],
        compiler_params=params(32),
        name="pack",
    )(*(pltpu.with_memory_space_constraint(x, pltpu.HBM) for x in operands))
    received = exchange(packed, devices)
    results = pl.pallas_call(
        functools.partial(convolve_kernel, parts, blocks, per),
        out_shape=jax.ShapeDtypeStruct((3 * channels * pieces, LANES), jnp.float32),
        compiler_params=params(48),
        name="convolve",
    )(received, *tables(blocks, rows))
    returned = exchange(results, devices)
    narrow = jax.ShapeDtypeStruct((rows, channels), jnp.bfloat16)
    wide = jax.ShapeDtypeStruct((rows, channels), jnp.float32)
    return pl.pallas_call(
        functools.partial(unpack_kernel, devices, 1.0 / math.sqrt(blocks * rows)),
        out_shape=(narrow, narrow, narrow, wide),
        in_specs=[in_vmem] * 4,
        out_specs=[in_hbm] * 4,
        scratch_shapes=[gate] * 3
        + [pltpu.VMEM((rows, channels), jnp.float32), pltpu.SemaphoreType.DMA((4, pieces))],
        compiler_params=params(32),
        name="unpack",
    )(returned, key_gate, value_seq, grad_output)


def solution(mesh):
    split_rows = P(ALL_AXES, None)
    return jax.shard_map(
        per_device,
        mesh=mesh,
        in_specs=(split_rows, split_rows, split_rows, split_rows, P(BLOCK_AXES, None)),
        out_specs=(split_rows, split_rows, split_rows, split_rows),
        check_vma=False,
    )
```

time: 71.8 us -> 71 us (0.989)
  no operation moved by 1% of the time
where the time goes in v3:
time: 71 us; the launch traced here: 70.8 us
  blocking collectives  62.2 us (88%)
  Pallas kernels  7.95 us (11%)
    all_to_all x2, blocking collectives, exchange(): lax.all_to_all(slabs, ALL_AXES, split_axis=0, concat_axis=0, tiled=True)  62.2 us
    pallas_call x1, Pallas kernels, per_device(): pl.pallas_call(functools.partial(convolve_kernel, parts, blocks, per), ou...  5.03 us
    pallas_call x1, Pallas kernels, per_device(): pl.pallas_call(functools.partial(pack_kernel, parts, devices), out_shape=...  1.62 us

profile of v3, /device:TPU:1, one launch (start us, length us, event | category | flops | bytes accessed | tf_op | source)
XLA Modules:
  0.0 70.8 jit_solution(6973198468411246147)
XLA Ops:
  0.6 1.6 %pack.1 = f32[2560,128]{1,0:T(8,128)S(1)} custom-call(bf16[512,256]{1,0:T(8,128)(2,1)} %key_ref.1, bf16[512,256]{1,0:T(8,128)(2,1)} %value_ref.1, bf16[512,256]{1,0:T(8,128)(2,1)} %grad_ref.1, bf16[512,256]{1,0:T(8,128)(2,1)} %query_hbm.1, f32[512,256]{1,0:T(8,128)} %taps_hbm.1), custom_call_target="tpu_custom_call" | custom-call | tf_op jit(solution)/shard_map/pack/pallas_call | solution.py:275
  2.3 0.0 copy-start
  2.3 0.0 copy-start.4
  2.3 33.2 %all_to_all.10 = f32[128,5,4,128]{3,2,1,0:T(4,128)S(1)} all-to-all(f32[128,5,4,128]{3,2,1,0:T(4,128)S(1)} %bitcast.7), channel_id=1, replica_groups=mesh['dp'=2,'outer'=4,'inner'=16] {'dp','outer','inner'}, dimensions={0} | all-to-all | bytes 2621440 | tf_op jit(solution)/shard_map/all_to_all | solution.py:259
  35.4 0.0 copy-done
  35.5 0.0 copy-done.4
  35.5 5.0 %convolve.1 = f32[3072,128]{1,0:T(8,128)S(1)} custom-call(f32[2560,128]{1,0:T(8,128)S(1)} %bitcast.6, bf16[3072,256]{1,0:T(8,128)(2,1)S(1)} %copy-done, f32[2,256,128]{2,1,0:T(8,128)S(1)} %copy-done.4), custom_call_target="tpu_custom_call" | custom-call | tf_op jit(solution)/shard_map/convolve/pallas_call | solution.py:286
  40.5 0.0 copy-start.1
  40.5 0.0 copy-start.2
  40.5 0.0 copy-start.3
  40.5 29.0 %all_to_all.11 = f32[128,6,4,128]{3,2,1,0:T(4,128)S(1)} all-to-all(f32[128,6,4,128]{3,2,1,0:T(4,128)S(1)} %bitcast.5), channel_id=1, replica_groups=mesh['dp'=2,'outer'=4,'inner'=16] {'dp','outer','inner'}, dimensions={0} | all-to-all | bytes 3145728 | tf_op jit(solution)/shard_map/all_to_all | solution.py:259
  69.5 0.0 copy-done.1
  69.5 0.0 copy-done.2
  69.5 0.0 copy-done.3
  69.5 1.3 %unpack.1 = (bf16[512,256]{1,0:T(8,128)(2,1)}, bf16[512,256]{1,0:T(8,128)(2,1)}, bf16[512,256]{1,0:T(8,128)(2,1)}, f32[512,256]{1,0:T(8,128)}) custom-call(f32[3072,128]{1,0:T(8,128)S(1)} %bitcast.4, bf16[512,256]{1,0:T(8,128)(2,1)S(1)} %copy-done.1, bf16[512,256]{1,0:T(8,128)(2,1)S(1)} %copy-done.2, bf16[512,256]{1,0:T(8,128)(2,1)S(1)} %copy-done.3), custom_call_target="tpu_custom_call" | custom-call | tf_op jit(solution)/shard_map/unpack/pallas_call | solution.py:295
Async XLA Ops:
  2.3 33.2 %copy-start = (bf16[3072,256]{1,0:T(8,128)(2,1)S(1)}, bf16[3072,256]{1,0:T(8,128)(2,1)}, u32[]{:S(2)}) copy-start(bf16[3072,256]{1,0:T(8,128)(2,1)} %constant.4.clone.tables_ref) | copy-start | bytes 4718596
  2.3 33.2 %copy-start.4 = (f32[2,256,128]{2,1,0:T(8,128)S(1)}, f32[2,256,128]{2,1,0:T(8,128)}, u32[]{:S(2)}) copy-start(f32[2,256,128]{2,1,0:T(8,128)} %constant.5.clone.twist_ref) | copy-start | bytes 786436
  40.5 29.0 %copy-start.1 = (bf16[512,256]{1,0:T(8,128)(2,1)S(1)}, bf16[512,256]{1,0:T(8,128)(2,1)}, u32[]{:S(2)}) copy-start(bf16[512,256]{1,0:T(8,128)(2,1)} %key_ref.1) | copy-start | bytes 786436
  40.5 29.0 %copy-start.2 = (bf16[512,256]{1,0:T(8,128)(2,1)S(1)}, bf16[512,256]{1,0:T(8,128)(2,1)}, u32[]{:S(2)}) copy-start(bf16[512,256]{1,0:T(8,128)(2,1)} %value_ref.1) | copy-start | bytes 786436
  40.5 29.0 %copy-start.3 = (bf16[512,256]{1,0:T(8,128)(2,1)S(1)}, bf16[512,256]{1,0:T(8,128)(2,1)}, u32[]{:S(2)}) copy-start(bf16[512,256]{1,0:T(8,128)(2,1)} %grad_ref.1) | copy-start | bytes 786436

commit v4 on v3

--- a/solution.py
+++ b/solution.py
@@ -21,34 +21,28 @@
     return high, low
 
 
-def square_table(table):
+def tall_table(table):
     high, low = split_table(table)
-    return np.block([[high, low], [high, np.zeros_like(low)]])
+    return np.concatenate([high, low, high], axis=0)
 
 
 def tables(groups, width):
     pieces = width // LANES
     n1 = groups * pieces
     length = n1 * LANES
-    order = (np.arange(groups)[None, :] * pieces + np.arange(pieces)[:, None]).reshape(-1)
-    k1 = np.arange(n1) + 0.25
-    turn = (k1[:, None] * order[None, :]) * (2.0 * math.pi / n1)
-    outer = np.concatenate([np.cos(turn), -np.sin(turn)], axis=0)
-    back_outer = np.concatenate([np.cos(turn.T), -np.sin(turn.T)], axis=1) / length
-    twist = k1[:, None] * np.arange(LANES)[None, :] * (2.0 * math.pi / length)
-    half = np.arange(LANES // 2)
-    even = half[:, None] * half[None, :] * (4.0 * math.pi / LANES)
-    odd = half[:, None] * (2 * half[None, :] + 1) * (2.0 * math.pi / LANES)
-    inner_even = np.block([[np.cos(even), -np.sin(even)], [np.sin(even), np.cos(even)]])
-    inner_odd = np.block([[np.cos(odd), -np.sin(odd)], [-np.sin(odd), -np.cos(odd)]])
-    back_even = np.block([[np.cos(even.T), np.sin(even.T)], [-np.sin(even.T), np.cos(even.T)]])
-    back_odd = np.block([[np.cos(odd.T), np.sin(odd.T)], [-np.sin(odd.T), np.cos(odd.T)]])
-    back_high, back_low = split_table(back_outer)
-    narrow = [
-        *split_table(outer),
-        *(half for whole in (back_high, back_low) for half in np.split(whole, 2, axis=1)),
-        *(square_table(t) for t in (inner_even, inner_odd, back_even, back_odd)),
-    ]
+    group, low = np.arange(groups), np.arange(groups) + 0.25
+    narrow, back = [], []
+    for piece in range(pieces):
+        turn = low[:, None] * (group[None, :] / groups + piece / n1) * (2.0 * math.pi)
+        high_part, low_part = split_table(np.concatenate([np.cos(turn), -np.sin(turn)], axis=0))
+        narrow.append(np.block([[high_part, high_part, low_part, low_part]]))
+        high_part, low_part = split_table(np.concatenate([np.cos(turn.T), -np.sin(turn.T)], axis=1) / length)
+        back.append(np.block([[high_part, high_part], [low_part, low_part]]))
+    twist = (np.arange(n1) + 0.25)[:, None] * np.arange(LANES)[None, :] * (2.0 * math.pi / length)
+    lane = np.arange(LANES)
+    spin = lane[:, None] * lane[None, :] * (2.0 * math.pi / LANES)
+    cos, sin = np.cos(spin), np.sin(spin)
+    narrow += back + [tall_table(np.block([[cos, -sin], [sin, cos]])), tall_table(np.block([[cos, sin], [-sin, cos]]))]
     return np.concatenate(narrow, axis=0), np.stack([np.cos(twist), np.sin(twist)]).astype(np.float32)
 
 
@@ -58,15 +52,9 @@
     return high, low
 
 
-def dot3(left, right):
-    wide = jnp.concatenate([left[0], left[1], left[0]], axis=1)
-    tall = jnp.concatenate([right[0], right[0], right[1]], axis=0)
-    return jnp.dot(wide, tall, preferred_element_type=jnp.float32)
-
-
-def dot_square(value, table):
-    sums = jnp.dot(jnp.concatenate(split(value), axis=1), table, preferred_element_type=jnp.float32)
-    return sums[:, :LANES] + sums[:, LANES:]
+def dot_wide(value, table):
+    high, low = split(value)
+    return jnp.dot(jnp.concatenate([high, high, low], axis=1), table, preferred_element_type=jnp.float32)
 
 
 def pack_kernel(
@@ -141,82 +129,81 @@
     taps_pieces = pieces // parts
     slab_in = per * (2 * pieces + taps_pieces)
     slab_out = 3 * per * pieces
-    square = 2 * LANES
+    tall = 6 * LANES
 
     def table(start, rows):
         return tables_ref[start : start + rows, :]
 
-    def wide_table(start):
-        return jnp.concatenate([table(start, n1), table(start + n1, n1)], axis=1)
-
-    outer = (table(0, 2 * n1), table(2 * n1, 2 * n1))
-    back_outer = (wide_table(4 * n1), wide_table(6 * n1))
-    even, odd, back_even, back_odd = (table(8 * n1 + n * square, square) for n in range(4))
-
-    def first_half(left, right):
-        lane = lax.broadcasted_iota(jnp.int32, left.shape, 1)
-        return jnp.where(lane < LANES // 2, left, right)
-
-    def swap(value):
-        return pltpu.roll(value, LANES // 2, 1)
+    outer = [table(piece * LANES, LANES) for piece in range(pieces)]
+    back_outer = [table((pieces + piece) * LANES, LANES) for piece in range(pieces)]
+    inner, back_inner = (table(2 * pieces * LANES + n * tall, tall) for n in range(2))
 
     def load(row, part):
         return in_ref[pl.ds(part * blocks * slab_in + row, blocks, stride=slab_in), :]
 
     def load_signal(s, c, part):
-        return jnp.concatenate([load((s * per + c) * pieces + piece, part) for piece in range(pieces)], axis=0)
+        return [load((s * per + c) * pieces + piece, part) for piece in range(pieces)]
 
     def load_taps(c):
-        first = (2 * pieces * per) + c * taps_pieces
-        return jnp.concatenate(
-            [load(first + piece % taps_pieces, piece // taps_pieces) for piece in range(pieces)], axis=0
+        first = 2 * pieces * per + c * taps_pieces
+        return [load(first + piece % taps_pieces, piece // taps_pieces) for piece in range(pieces)]
+
+    def butterfly(first, second, third, fourth, sign):
+        sums = [a + b for a, b in zip(first, third)], [a + b for a, b in zip(second, fourth)]
+        differences = [a - b for a, b in zip(first, third)], [a - b for a, b in zip(second, fourth)]
+        (near_re, near_im), (far_re, far_im) = differences
+        turned = [near_re - far_im, near_im + far_re], [near_re + far_im, near_im - far_re]
+        return (
+            [a + b for a, b in zip(*sums)],
+            turned[0] if sign > 0 else turned[1],
+            [a - b for a, b in zip(*sums)],
+            turned[1] if sign > 0 else turned[0],
         )
 
     def outer_step(signals):
-        mixed = dot3(outer, split(jnp.concatenate(signals, axis=1)))
-        ups, downs = [], []
+        parts_of = []
+        for piece in range(pieces):
+            high, low = split(jnp.concatenate([signal[piece] for signal in signals], axis=1))
+            tall = jnp.concatenate([high, low, high, low], axis=0)
+            sums = jnp.dot(outer[piece], tall, preferred_element_type=jnp.float32)
+            parts_of.append((sums[:blocks], sums[blocks:]))
+        spectra = butterfly(*parts_of, -1)
+        turned = []
         for n in range(len(signals)):
             lanes = slice(n * LANES, (n + 1) * LANES)
-            re, im = mixed[:n1, lanes], mixed[n1:, lanes]
+            re, im = (jnp.concatenate([one[half][:, lanes] for one in spectra], axis=0) for half in range(2))
             cos, sin = twist_ref[0], twist_ref[1]
-            re, im = re * cos + im * sin, im * cos - re * sin
-            near, far = first_half(re, im), swap(first_half(im, re))
-            ups.append(near + far)
-            downs.append(near - far)
-        return jnp.concatenate(ups, axis=0), jnp.concatenate(downs, axis=0)
+            turned.append(jnp.concatenate([re * cos + im * sin, im * cos - re * sin], axis=1))
+        return jnp.concatenate(turned, axis=0)
 
     def inner_step(turned):
-        spectra = (dot_square(turned[0], even), dot_square(turned[1], odd))
-        return [(one, swap(one)) for one in spectra]
-
-    def factors(spectra):
-        return [(first_half(one, other), first_half(-other, one)) for one, other in spectra]
+        done = dot_wide(turned, inner)
+        return done[:, :LANES], done[:, LANES:]
 
     def product(left, right):
-        return [one * re + other * im for (one, other), (re, im) in zip(left, right)]
+        return [left[0] * right[0] - left[1] * right[1], left[0] * right[1] + left[1] * right[0]]
 
     def product_conjugate(left, right):
-        return [one * re - other * im for (one, other), (re, im) in zip(left, right)]
+        return [left[0] * right[0] + left[1] * right[1], left[1] * right[0] - left[0] * right[1]]
 
     def back_inner_step(products):
-        sums_even, sums_odd = dot_square(products[0], back_even), dot_square(products[1], back_odd)
-        near, far = sums_even + sums_odd, sums_even - sums_odd
-        turned = swap(first_half(far, near))
-        res, ims = first_half(near, turned), first_half(turned, far)
+        done = dot_wide(jnp.concatenate(products, axis=1), back_inner)
         columns = []
         for n in range(parts):
-            re, im = res[n * n1 : (n + 1) * n1], ims[n * n1 : (n + 1) * n1]
+            re, im = done[n * n1 : (n + 1) * n1, :LANES], done[n * n1 : (n + 1) * n1, LANES:]
             cos, sin = twist_ref[0], twist_ref[1]
-            columns.append(jnp.concatenate([re * cos - im * sin, re * sin + im * cos], axis=0))
-        return jnp.concatenate(columns, axis=1)
+            columns.append((re * cos - im * sin, re * sin + im * cos))
+        return [jnp.concatenate(halves, axis=1) for halves in zip(*columns)]
 
     def back_outer_step(s, c, columns):
-        signals = dot3(back_outer, split(columns))
-        for part in range(parts):
-            for piece in range(pieces):
+        quarters = ([half[n * blocks : (n + 1) * blocks] for half in columns] for n in range(pieces))
+        for piece, turned in enumerate(butterfly(*quarters, 1)):
+            tall = jnp.concatenate(split(jnp.concatenate(turned, axis=0)), axis=0)
+            sums = jnp.dot(back_outer[piece], tall, preferred_element_type=jnp.float32)
+            signals = sums[:blocks] + sums[blocks:]
+            for part in range(parts):
                 row = part * blocks * slab_out + (s * per + c) * pieces + piece
-                block = signals[piece * blocks : (piece + 1) * blocks, part * LANES : (part + 1) * LANES]
-                out_ref[pl.ds(row, blocks, stride=slab_out), :] = block
+                out_ref[pl.ds(row, blocks, stride=slab_out), :] = signals[:, part * LANES : (part + 1) * LANES]
 
     def signal(s, c):
         return [load_signal(s, c, part) for part in range(parts)]
@@ -225,29 +212,29 @@
         one = pair[c * n1 : (c + 1) * n1]
         return jnp.concatenate([one] * parts, axis=0)
 
+    t = outer_step([load_taps(c) for c in range(per)])
     m0 = outer_step(signal(0, 0))
     g0 = outer_step(signal(1, 0))
-    t = outer_step([load_taps(c) for c in range(per)])
+    t = inner_step(t)
+    taps = [[channel(half, c) for half in t] for c in range(per)]
     m0 = inner_step(m0)
+    m1 = outer_step(signal(0, 1))
     g0 = inner_step(g0)
-    t = factors(inner_step(t))
-    taps = [[tuple(channel(f, c) for f in half) for half in t] for c in range(per)]
-    m1 = outer_step(signal(0, 1))
+    conv0 = back_inner_step(product(m0, taps[0]))
     g1 = outer_step(signal(1, 1))
-    cross0 = back_inner_step(product_conjugate(g0, factors(m0)))
-    conv0 = back_inner_step(product(m0, taps[0]))
     corr0 = back_inner_step(product_conjugate(g0, taps[0]))
+    back_outer_step(0, 0, conv0)
+    cross0 = back_inner_step(product_conjugate(g0, m0))
+    m1 = inner_step(m1)
+    back_outer_step(1, 0, corr0)
     back_outer_step(2, 0, cross0)
-    back_outer_step(0, 0, conv0)
-    back_outer_step(1, 0, corr0)
-    m1 = inner_step(m1)
     g1 = inner_step(g1)
-    cross1 = back_inner_step(product_conjugate(g1, factors(m1)))
     conv1 = back_inner_step(product(m1, taps[1]))
     corr1 = back_inner_step(product_conjugate(g1, taps[1]))
-    back_outer_step(2, 1, cross1)
+    cross1 = back_inner_step(product_conjugate(g1, m1))
     back_outer_step(0, 1, conv1)
     back_outer_step(1, 1, corr1)
+    back_outer_step(2, 1, cross1)
 
 
 def params(size):

time: 71 us -> 70.2 us (0.989)
  Pallas kernels: 7.95 us -> 7.09 us
    pallas_call x1, Pallas kernels: 5.03 us -> 4.17 us  [per_device(): pl.pallas_call(functools.partial(convolve_kernel, parts, blocks, per), ou...]
where the time goes in v4:
time: 70.2 us; the launch traced here: 70 us
  blocking collectives  62.2 us (89%)
  Pallas kernels  7.09 us (10%)
    all_to_all x2, blocking collectives, exchange(): lax.all_to_all(slabs, ALL_AXES, split_axis=0, concat_axis=0, tiled=True)  62.2 us
    pallas_call x1, Pallas kernels, per_device(): pl.pallas_call(functools.partial(convolve_kernel, parts, blocks, per), ou...  4.17 us
    pallas_call x1, Pallas kernels, per_device(): pl.pallas_call(functools.partial(pack_kernel, parts, devices), out_shape=...  1.62 us

profile of v4, /device:TPU:1, one launch (start us, length us, event | category | flops | bytes accessed | tf_op | source)
XLA Modules:
  0.0 70.0 jit_solution(1642004666260157333)
XLA Ops:
  0.6 1.6 %pack.1 = f32[2560,128]{1,0:T(8,128)S(1)} custom-call(bf16[512,256]{1,0:T(8,128)(2,1)} %key_ref.1, bf16[512,256]{1,0:T(8,128)(2,1)} %value_ref.1, bf16[512,256]{1,0:T(8,128)(2,1)} %grad_ref.1, bf16[512,256]{1,0:T(8,128)(2,1)} %query_hbm.1, f32[512,256]{1,0:T(8,128)} %taps_hbm.1), custom_call_target="tpu_custom_call" | custom-call | tf_op jit(solution)/shard_map/pack/pallas_call | solution.py:262
  2.3 0.0 copy-start
  2.3 0.0 copy-start.4
  2.3 33.2 %all_to_all.10 = f32[128,5,4,128]{3,2,1,0:T(4,128)S(1)} all-to-all(f32[128,5,4,128]{3,2,1,0:T(4,128)S(1)} %bitcast.6), channel_id=1, replica_groups=mesh['dp'=2,'outer'=4,'inner'=16] {'dp','outer','inner'}, dimensions={0} | all-to-all | bytes 2621440 | tf_op jit(solution)/shard_map/all_to_all | solution.py:246
  35.4 0.0 copy-done
  35.5 0.0 copy-done.4
  35.5 4.2 %convolve.1 = f32[3072,128]{1,0:T(8,128)S(1)} custom-call(f32[2560,128]{1,0:T(8,128)S(1)} %bitcast.7, bf16[2560,256]{1,0:T(8,128)(2,1)S(1)} %copy-done, f32[2,256,128]{2,1,0:T(8,128)S(1)} %copy-done.4), custom_call_target="tpu_custom_call" | custom-call | tf_op jit(solution)/shard_map/convolve/pallas_call | solution.py:273
  39.6 0.0 copy-start.1
  39.6 0.0 copy-start.2
  39.7 0.0 copy-start.3
  39.7 29.0 %all_to_all.11 = f32[128,6,4,128]{3,2,1,0:T(4,128)S(1)} all-to-all(f32[128,6,4,128]{3,2,1,0:T(4,128)S(1)} %bitcast.5), channel_id=1, replica_groups=mesh['dp'=2,'outer'=4,'inner'=16] {'dp','outer','inner'}, dimensions={0} | all-to-all | bytes 3145728 | tf_op jit(solution)/shard_map/all_to_all | solution.py:246
  68.7 0.0 copy-done.1
  68.7 0.0 copy-done.2
  68.7 0.0 copy-done.3
  68.7 1.3 %unpack.1 = (bf16[512,256]{1,0:T(8,128)(2,1)}, bf16[512,256]{1,0:T(8,128)(2,1)}, bf16[512,256]{1,0:T(8,128)(2,1)}, f32[512,256]{1,0:T(8,128)}) custom-call(f32[3072,128]{1,0:T(8,128)S(1)} %bitcast.4, bf16[512,256]{1,0:T(8,128)(2,1)S(1)} %copy-done.1, bf16[512,256]{1,0:T(8,128)(2,1)S(1)} %copy-done.2, bf16[512,256]{1,0:T(8,128)(2,1)S(1)} %copy-done.3), custom_call_target="tpu_custom_call" | custom-call | tf_op jit(solution)/shard_map/unpack/pallas_call | solution.py:282
Async XLA Ops:
  2.3 33.2 %copy-start = (bf16[2560,256]{1,0:T(8,128)(2,1)S(1)}, bf16[2560,256]{1,0:T(8,128)(2,1)}, u32[]{:S(2)}) copy-start(bf16[2560,256]{1,0:T(8,128)(2,1)} %constant.4.clone.tables_ref) | copy-start | bytes 3932164
  2.3 33.2 %copy-start.4 = (f32[2,256,128]{2,1,0:T(8,128)S(1)}, f32[2,256,128]{2,1,0:T(8,128)}, u32[]{:S(2)}) copy-start(f32[2,256,128]{2,1,0:T(8,128)} %constant.5.clone.twist_ref) | copy-start | bytes 786436
  39.6 29.0 %copy-start.1 = (bf16[512,256]{1,0:T(8,128)(2,1)S(1)}, bf16[512,256]{1,0:T(8,128)(2,1)}, u32[]{:S(2)}) copy-start(bf16[512,256]{1,0:T(8,128)(2,1)} %key_ref.1) | copy-start | bytes 786436
  39.6 29.0 %copy-start.2 = (bf16[512,256]{1,0:T(8,128)(2,1)S(1)}, bf16[512,256]{1,0:T(8,128)(2,1)}, u32[]{:S(2)}) copy-start(bf16[512,256]{1,0:T(8,128)(2,1)} %value_ref.1) | copy-start | bytes 786436
  39.7 29.0 %copy-start.3 = (bf16[512,256]{1,0:T(8,128)(2,1)S(1)}, bf16[512,256]{1,0:T(8,128)(2,1)}, u32[]{:S(2)}) copy-start(bf16[512,256]{1,0:T(8,128)(2,1)} %grad_ref.1) | copy-start | bytes 786436

commit v5 on v4

--- a/solution.py
+++ b/solution.py
@@ -42,8 +42,9 @@
     lane = np.arange(LANES)
     spin = lane[:, None] * lane[None, :] * (2.0 * math.pi / LANES)
     cos, sin = np.cos(spin), np.sin(spin)
-    narrow += back + [tall_table(np.block([[cos, -sin], [sin, cos]])), tall_table(np.block([[cos, sin], [-sin, cos]]))]
-    return np.concatenate(narrow, axis=0), np.stack([np.cos(twist), np.sin(twist)]).astype(np.float32)
+    narrow += back + [tall_table(np.block([[cos, -sin], [sin, cos]]))]
+    back_inner = np.block([[cos, sin], [-sin, cos]]).astype(np.float32)
+    return np.concatenate(narrow, axis=0), back_inner, np.stack([np.cos(twist), np.sin(twist)]).astype(np.float32)
 
 
 def split(value):
@@ -123,20 +124,19 @@
         move.wait()
 
 
-def convolve_kernel(parts, blocks, per, in_ref, tables_ref, twist_ref, out_ref):
+def convolve_kernel(parts, blocks, per, in_ref, tables_ref, back_inner_ref, twist_ref, out_ref):
     n1 = twist_ref.shape[1]
     pieces = n1 // blocks
     taps_pieces = pieces // parts
     slab_in = per * (2 * pieces + taps_pieces)
     slab_out = 3 * per * pieces
-    tall = 6 * LANES
 
     def table(start, rows):
         return tables_ref[start : start + rows, :]
 
     outer = [table(piece * LANES, LANES) for piece in range(pieces)]
     back_outer = [table((pieces + piece) * LANES, LANES) for piece in range(pieces)]
-    inner, back_inner = (table(2 * pieces * LANES + n * tall, tall) for n in range(2))
+    inner = table(2 * pieces * LANES, 6 * LANES)
 
     def load(row, part):
         return in_ref[pl.ds(part * blocks * slab_in + row, blocks, stride=slab_in), :]
@@ -187,7 +187,12 @@
         return [left[0] * right[0] + left[1] * right[1], left[1] * right[0] - left[0] * right[1]]
 
     def back_inner_step(products):
-        done = dot_wide(jnp.concatenate(products, axis=1), back_inner)
+        done = jnp.dot(
+            jnp.concatenate(products, axis=1),
+            back_inner_ref[...],
+            precision=lax.Precision.HIGH,
+            preferred_element_type=jnp.float32,
+        )
         columns = []
         for n in range(parts):
             re, im = done[n * n1 : (n + 1) * n1, :LANES], done[n * n1 : (n + 1) * n1, LANES:]
@@ -217,8 +222,8 @@
     g0 = outer_step(signal(1, 0))
     t = inner_step(t)
     taps = [[channel(half, c) for half in t] for c in range(per)]
+    m1 = outer_step(signal(0, 1))
     m0 = inner_step(m0)
-    m1 = outer_step(signal(0, 1))
     g0 = inner_step(g0)
     conv0 = back_inner_step(product(m0, taps[0]))
     g1 = outer_step(signal(1, 1))
@@ -227,8 +232,8 @@
     cross0 = back_inner_step(product_conjugate(g0, m0))
     m1 = inner_step(m1)
     back_outer_step(1, 0, corr0)
+    g1 = inner_step(g1)
     back_outer_step(2, 0, cross0)
-    g1 = inner_step(g1)
     conv1 = back_inner_step(product(m1, taps[1]))
     corr1 = back_inner_step(product_conjugate(g1, taps[1]))
     cross1 = back_inner_step(product_conjugate(g1, m1))

time: 70.2 us -> 70.1 us (level)
  no operation moved by 1% of the time
where the time goes in v5:
time: 70.1 us; the launch traced here: 69.9 us
  blocking collectives  62.2 us (89%)
  Pallas kernels  7.03 us (10%)
    all_to_all x2, blocking collectives, exchange(): lax.all_to_all(slabs, ALL_AXES, split_axis=0, concat_axis=0, tiled=True)  62.2 us
    pallas_call x1, Pallas kernels, per_device(): pl.pallas_call(functools.partial(convolve_kernel, parts, blocks, per), ou...  4.11 us
    pallas_call x1, Pallas kernels, per_device(): pl.pallas_call(functools.partial(pack_kernel, parts, devices), out_shape=...  1.62 us

profile of v5, /device:TPU:1, one launch (start us, length us, event | category | flops | bytes accessed | tf_op | source)
XLA Modules:
  0.0 69.9 jit_solution(17862728113849795202)
XLA Ops:
  0.6 1.6 %pack.1 = f32[2560,128]{1,0:T(8,128)S(1)} custom-call(bf16[512,256]{1,0:T(8,128)(2,1)} %key_ref.1, bf16[512,256]{1,0:T(8,128)(2,1)} %value_ref.1, bf16[512,256]{1,0:T(8,128)(2,1)} %grad_ref.1, bf16[512,256]{1,0:T(8,128)(2,1)} %query_hbm.1, f32[512,256]{1,0:T(8,128)} %taps_hbm.1), custom_call_target="tpu_custom_call" | custom-call | tf_op jit(solution)/shard_map/pack/pallas_call | solution.py:267
  2.3 0.0 copy-start.3
  2.3 0.0 copy-start.4
  2.3 0.0 copy-start.5
  2.3 33.2 %all_to_all.10 = f32[128,5,4,128]{3,2,1,0:T(4,128)S(1)} all-to-all(f32[128,5,4,128]{3,2,1,0:T(4,128)S(1)} %bitcast.7), channel_id=1, replica_groups=mesh['dp'=2,'outer'=4,'inner'=16] {'dp','outer','inner'}, dimensions={0} | all-to-all | bytes 2621440 | tf_op jit(solution)/shard_map/all_to_all | solution.py:251
  35.5 0.0 copy-done.3
  35.5 0.0 copy-done.4
  35.5 0.0 copy-done.5
  35.5 4.1 %convolve.1 = f32[3072,128]{1,0:T(8,128)S(1)} custom-call(f32[2560,128]{1,0:T(8,128)S(1)} %bitcast.6, bf16[1792,256]{1,0:T(8,128)(2,1)S(1)} %copy-done.3, f32[256,256]{1,0:T(8,128)S(1)} %copy-done.5, f32[2,256,128]{2,1,0:T(8,128)S(1)} %copy-done.4), custom_call_target="tpu_custom_call" | custom-call | tf_op jit(solution)/shard_map/convolve/pallas_call | solution.py:278
  39.6 0.0 copy-start
  39.6 0.0 copy-start.1
  39.6 0.0 copy-start.2
  39.6 29.0 %all_to_all.11 = f32[128,6,4,128]{3,2,1,0:T(4,128)S(1)} all-to-all(f32[128,6,4,128]{3,2,1,0:T(4,128)S(1)} %bitcast.5), channel_id=1, replica_groups=mesh['dp'=2,'outer'=4,'inner'=16] {'dp','outer','inner'}, dimensions={0} | all-to-all | bytes 3145728 | tf_op jit(solution)/shard_map/all_to_all | solution.py:251
  68.6 0.0 copy-done
  68.6 0.0 copy-done.1
  68.6 0.0 copy-done.2
  68.6 1.3 %unpack.1 = (bf16[512,256]{1,0:T(8,128)(2,1)}, bf16[512,256]{1,0:T(8,128)(2,1)}, bf16[512,256]{1,0:T(8,128)(2,1)}, f32[512,256]{1,0:T(8,128)}) custom-call(f32[3072,128]{1,0:T(8,128)S(1)} %bitcast.4, bf16[512,256]{1,0:T(8,128)(2,1)S(1)} %copy-done, bf16[512,256]{1,0:T(8,128)(2,1)S(1)} %copy-done.1, bf16[512,256]{1,0:T(8,128)(2,1)S(1)} %copy-done.2), custom_call_target="tpu_custom_call" | custom-call | tf_op jit(solution)/shard_map/unpack/pallas_call | solution.py:287
Async XLA Ops:
  2.3 33.2 %copy-start.3 = (bf16[1792,256]{1,0:T(8,128)(2,1)S(1)}, bf16[1792,256]{1,0:T(8,128)(2,1)}, u32[]{:S(2)}) copy-start(bf16[1792,256]{1,0:T(8,128)(2,1)} %constant.6.clone.tables_ref) | copy-start | bytes 2752516
  2.3 33.2 %copy-start.4 = (f32[2,256,128]{2,1,0:T(8,128)S(1)}, f32[2,256,128]{2,1,0:T(8,128)}, u32[]{:S(2)}) copy-start(f32[2,256,128]{2,1,0:T(8,128)} %constant.8.clone.twist_ref) | copy-start | bytes 786436
  2.3 33.2 %copy-start.5 = (f32[256,256]{1,0:T(8,128)S(1)}, f32[256,256]{1,0:T(8,128)}, u32[]{:S(2)}) copy-start(f32[256,256]{1,0:T(8,128)} %constant.7.clone.back_inner_ref) | copy-start | bytes 786436
  39.6 29.0 %copy-start = (bf16[512,256]{1,0:T(8,128)(2,1)S(1)}, bf16[512,256]{1,0:T(8,128)(2,1)}, u32[]{:S(2)}) copy-start(bf16[512,256]{1,0:T(8,128)(2,1)} %key_ref.1) | copy-start | bytes 786436
  39.6 29.0 %copy-start.1 = (bf16[512,256]{1,0:T(8,128)(2,1)S(1)}, bf16[512,256]{1,0:T(8,128)(2,1)}, u32[]{:S(2)}) copy-start(bf16[512,256]{1,0:T(8,128)(2,1)} %value_ref.1) | copy-start | bytes 786436
  39.6 29.0 %copy-start.2 = (bf16[512,256]{1,0:T(8,128)(2,1)S(1)}, bf16[512,256]{1,0:T(8,128)(2,1)}, u32[]{:S(2)}) copy-start(bf16[512,256]{1,0:T(8,128)(2,1)} %grad_ref.1) | copy-start | bytes 786436

commit v6 on v4

--- a/solution.py
+++ b/solution.py
@@ -78,17 +78,17 @@
             span = slice(piece * LANES, (piece + 1) * LANES)
             put(left[span, :].astype(jnp.float32) * right[span, :].astype(jnp.float32), first, pieces, piece)
 
-    sources = (key_hbm, value_hbm, taps_hbm.at[pl.ds(start, taps_rows), :], grad_hbm, query_hbm)
-    targets = (key, value, taps, grad, query)
+    sources = (taps_hbm.at[pl.ds(start, taps_rows), :], key_hbm, value_hbm, grad_hbm, query_hbm)
+    targets = (taps, key, value, grad, query)
     moves = [pltpu.make_async_copy(src, dst, sems.at[n]) for n, (src, dst) in enumerate(zip(sources, targets))]
     for move in moves:
         move.start()
     moves[0].wait()
-    moves[1].wait()
-    put_product(key, value, 0)
-    moves[2].wait()
     for piece in range(taps_pieces):
         put(taps[piece * LANES : (piece + 1) * LANES, :], 2 * per * pieces, taps_pieces, piece)
+    moves[1].wait()
+    moves[2].wait()
+    put_product(key, value, 0)
     moves[3].wait()
     moves[4].wait()
     put_product(grad, query, per * pieces)

time: 70.2 us -> 70.1 us (level)
  no operation moved by 1% of the time
where the time goes in v6:
time: 70.1 us; the launch traced here: 69.9 us
  blocking collectives  62.2 us (89%)
  Pallas kernels  7.04 us (10%)
    all_to_all x2, blocking collectives, exchange(): lax.all_to_all(slabs, ALL_AXES, split_axis=0, concat_axis=0, tiled=True)  62.2 us
    pallas_call x1, Pallas kernels, per_device(): pl.pallas_call(functools.partial(convolve_kernel, parts, blocks, per), ou...  4.17 us
    pallas_call x1, Pallas kernels, per_device(): pl.pallas_call(functools.partial(pack_kernel, parts, devices), out_shape=...  1.57 us

profile of v6, /device:TPU:1, one launch (start us, length us, event | category | flops | bytes accessed | tf_op | source)
XLA Modules:
  0.0 69.9 jit_solution(6050014979485308135)
XLA Ops:
  0.6 1.6 %pack.1 = f32[2560,128]{1,0:T(8,128)S(1)} custom-call(bf16[512,256]{1,0:T(8,128)(2,1)} %key_ref.1, bf16[512,256]{1,0:T(8,128)(2,1)} %value_ref.1, bf16[512,256]{1,0:T(8,128)(2,1)} %grad_ref.1, bf16[512,256]{1,0:T(8,128)(2,1)} %query_hbm.1, f32[512,256]{1,0:T(8,128)} %taps_hbm.1), custom_call_target="tpu_custom_call" | custom-call | tf_op jit(solution)/shard_map/pack/pallas_call | solution.py:262
  2.2 0.0 copy-start
  2.2 0.0 copy-start.4
  2.2 33.2 %all_to_all.10 = f32[128,5,4,128]{3,2,1,0:T(4,128)S(1)} all-to-all(f32[128,5,4,128]{3,2,1,0:T(4,128)S(1)} %bitcast.6), channel_id=1, replica_groups=mesh['dp'=2,'outer'=4,'inner'=16] {'dp','outer','inner'}, dimensions={0} | all-to-all | bytes 2621440 | tf_op jit(solution)/shard_map/all_to_all | solution.py:246
  35.4 0.0 copy-done
  35.4 0.0 copy-done.4
  35.4 4.2 %convolve.1 = f32[3072,128]{1,0:T(8,128)S(1)} custom-call(f32[2560,128]{1,0:T(8,128)S(1)} %bitcast.7, bf16[2560,256]{1,0:T(8,128)(2,1)S(1)} %copy-done, f32[2,256,128]{2,1,0:T(8,128)S(1)} %copy-done.4), custom_call_target="tpu_custom_call" | custom-call | tf_op jit(solution)/shard_map/convolve/pallas_call | solution.py:273
  39.6 0.0 copy-start.1
  39.6 0.0 copy-start.2
  39.6 0.0 copy-start.3
  39.6 29.0 %all_to_all.11 = f32[128,6,4,128]{3,2,1,0:T(4,128)S(1)} all-to-all(f32[128,6,4,128]{3,2,1,0:T(4,128)S(1)} %bitcast.5), channel_id=1, replica_groups=mesh['dp'=2,'outer'=4,'inner'=16] {'dp','outer','inner'}, dimensions={0} | all-to-all | bytes 3145728 | tf_op jit(solution)/shard_map/all_to_all | solution.py:246
  68.6 0.0 copy-done.1
  68.6 0.0 copy-done.2
  68.6 0.0 copy-done.3
  68.6 1.3 %unpack.1 = (bf16[512,256]{1,0:T(8,128)(2,1)}, bf16[512,256]{1,0:T(8,128)(2,1)}, bf16[512,256]{1,0:T(8,128)(2,1)}, f32[512,256]{1,0:T(8,128)}) custom-call(f32[3072,128]{1,0:T(8,128)S(1)} %bitcast.4, bf16[512,256]{1,0:T(8,128)(2,1)S(1)} %copy-done.1, bf16[512,256]{1,0:T(8,128)(2,1)S(1)} %copy-done.2, bf16[512,256]{1,0:T(8,128)(2,1)S(1)} %copy-done.3), custom_call_target="tpu_custom_call" | custom-call | tf_op jit(solution)/shard_map/unpack/pallas_call | solution.py:282
Async XLA Ops:
  2.2 33.2 %copy-start = (bf16[2560,256]{1,0:T(8,128)(2,1)S(1)}, bf16[2560,256]{1,0:T(8,128)(2,1)}, u32[]{:S(2)}) copy-start(bf16[2560,256]{1,0:T(8,128)(2,1)} %constant.4.clone.tables_ref) | copy-start | bytes 3932164
  2.2 33.2 %copy-start.4 = (f32[2,256,128]{2,1,0:T(8,128)S(1)}, f32[2,256,128]{2,1,0:T(8,128)}, u32[]{:S(2)}) copy-start(f32[2,256,128]{2,1,0:T(8,128)} %constant.5.clone.twist_ref) | copy-start | bytes 786436
  39.6 29.0 %copy-start.1 = (bf16[512,256]{1,0:T(8,128)(2,1)S(1)}, bf16[512,256]{1,0:T(8,128)(2,1)}, u32[]{:S(2)}) copy-start(bf16[512,256]{1,0:T(8,128)(2,1)} %key_ref.1) | copy-start | bytes 786436
  39.6 29.0 %copy-start.2 = (bf16[512,256]{1,0:T(8,128)(2,1)S(1)}, bf16[512,256]{1,0:T(8,128)(2,1)}, u32[]{:S(2)}) copy-start(bf16[512,256]{1,0:T(8,128)(2,1)} %value_ref.1) | copy-start | bytes 786436
  39.6 29.0 %copy-start.3 = (bf16[512,256]{1,0:T(8,128)(2,1)S(1)}, bf16[512,256]{1,0:T(8,128)(2,1)}, u32[]{:S(2)}) copy-start(bf16[512,256]{1,0:T(8,128)(2,1)} %grad_ref.1) | copy-start | bytes 786436

commit v7 on v4

--- a/solution.py
+++ b/solution.py
@@ -53,7 +53,7 @@
 
 
 def dot_wide(value, table):
-    high, low = split(value)
+    high, low = value
     return jnp.dot(jnp.concatenate([high, high, low], axis=1), table, preferred_element_type=jnp.float32)
 
 
@@ -160,45 +160,50 @@
             turned[1] if sign > 0 else turned[0],
         )
 
-    def outer_step(signals):
+    def outer_products(signals):
         parts_of = []
         for piece in range(pieces):
             high, low = split(jnp.concatenate([signal[piece] for signal in signals], axis=1))
             tall = jnp.concatenate([high, low, high, low], axis=0)
             sums = jnp.dot(outer[piece], tall, preferred_element_type=jnp.float32)
             parts_of.append((sums[:blocks], sums[blocks:]))
+        return parts_of
+
+    def outer_turns(parts_of):
         spectra = butterfly(*parts_of, -1)
         turned = []
-        for n in range(len(signals)):
+        for n in range(parts):
             lanes = slice(n * LANES, (n + 1) * LANES)
             re, im = (jnp.concatenate([one[half][:, lanes] for one in spectra], axis=0) for half in range(2))
             cos, sin = twist_ref[0], twist_ref[1]
             turned.append(jnp.concatenate([re * cos + im * sin, im * cos - re * sin], axis=1))
-        return jnp.concatenate(turned, axis=0)
-
-    def inner_step(turned):
+        return split(jnp.concatenate(turned, axis=0))
+
+    def inner_products(turned):
         done = dot_wide(turned, inner)
         return done[:, :LANES], done[:, LANES:]
 
     def product(left, right):
-        return [left[0] * right[0] - left[1] * right[1], left[0] * right[1] + left[1] * right[0]]
+        re, im = left[0] * right[0] - left[1] * right[1], left[0] * right[1] + left[1] * right[0]
+        return split(jnp.concatenate([re, im], axis=1))
 
     def product_conjugate(left, right):
-        return [left[0] * right[0] + left[1] * right[1], left[1] * right[0] - left[0] * right[1]]
-
-    def back_inner_step(products):
-        done = dot_wide(jnp.concatenate(products, axis=1), back_inner)
+        re, im = left[0] * right[0] + left[1] * right[1], left[1] * right[0] - left[0] * right[1]
+        return split(jnp.concatenate([re, im], axis=1))
+
+    def back_turns(done):
         columns = []
         for n in range(parts):
             re, im = done[n * n1 : (n + 1) * n1, :LANES], done[n * n1 : (n + 1) * n1, LANES:]
             cos, sin = twist_ref[0], twist_ref[1]
             columns.append((re * cos - im * sin, re * sin + im * cos))
-        return [jnp.concatenate(halves, axis=1) for halves in zip(*columns)]
-
-    def back_outer_step(s, c, columns):
-        quarters = ([half[n * blocks : (n + 1) * blocks] for half in columns] for n in range(pieces))
-        for piece, turned in enumerate(butterfly(*quarters, 1)):
-            tall = jnp.concatenate(split(jnp.concatenate(turned, axis=0)), axis=0)
+        halves = [jnp.concatenate(half, axis=1) for half in zip(*columns)]
+        quarters = ([half[n * blocks : (n + 1) * blocks] for half in halves] for n in range(pieces))
+        turns = butterfly(*quarters, 1)
+        return [jnp.concatenate(split(jnp.concatenate(turned, axis=0)), axis=0) for turned in turns]
+
+    def back_outer_products(s, c, talls):
+        for piece, tall in enumerate(talls):
             sums = jnp.dot(back_outer[piece], tall, preferred_element_type=jnp.float32)
             signals = sums[:blocks] + sums[blocks:]
             for part in range(parts):
@@ -212,29 +217,46 @@
         one = pair[c * n1 : (c + 1) * n1]
         return jnp.concatenate([one] * parts, axis=0)
 
-    t = outer_step([load_taps(c) for c in range(per)])
-    m0 = outer_step(signal(0, 0))
-    g0 = outer_step(signal(1, 0))
-    t = inner_step(t)
-    taps = [[channel(half, c) for half in t] for c in range(per)]
-    m0 = inner_step(m0)
-    m1 = outer_step(signal(0, 1))
-    g0 = inner_step(g0)
-    conv0 = back_inner_step(product(m0, taps[0]))
-    g1 = outer_step(signal(1, 1))
-    corr0 = back_inner_step(product_conjugate(g0, taps[0]))
-    back_outer_step(0, 0, conv0)
-    cross0 = back_inner_step(product_conjugate(g0, m0))
-    m1 = inner_step(m1)
-    back_outer_step(1, 0, corr0)
-    back_outer_step(2, 0, cross0)
-    g1 = inner_step(g1)
-    conv1 = back_inner_step(product(m1, taps[1]))
-    corr1 = back_inner_step(product_conjugate(g1, taps[1]))
-    cross1 = back_inner_step(product_conjugate(g1, m1))
-    back_outer_step(0, 1, conv1)
-    back_outer_step(1, 1, corr1)
-    back_outer_step(2, 1, cross1)
+    grad1 = outer_products(signal(1, 1))
+    mixed0 = outer_products(signal(0, 0))
+    grad1 = outer_turns(grad1)
+    grad0 = outer_products(signal(1, 0))
+    mixed0 = outer_turns(mixed0)
+    taps = outer_products([load_taps(c) for c in range(per)])
+    grad0 = outer_turns(grad0)
+    mixed1 = outer_products(signal(0, 1))
+    grad1 = inner_products(grad1)
+    taps = outer_turns(taps)
+    taps = inner_products(taps)
+    taps = [[channel(half, c) for half in taps] for c in range(per)]
+    corr1 = product_conjugate(grad1, taps[1])
+    mixed1 = outer_turns(mixed1)
+    mixed1 = inner_products(mixed1)
+    grad0 = inner_products(grad0)
+    conv1 = product(mixed1, taps[1])
+    cross1 = product_conjugate(grad1, mixed1)
+    mixed0 = inner_products(mixed0)
+    cross0 = product_conjugate(grad0, mixed0)
+    corr0 = product_conjugate(grad0, taps[0])
+    corr0 = dot_wide(corr0, back_inner)
+    cross0 = dot_wide(cross0, back_inner)
+    conv0 = product(mixed0, taps[0])
+    corr0 = back_turns(corr0)
+    corr1 = dot_wide(corr1, back_inner)
+    cross0 = back_turns(cross0)
+    conv1 = dot_wide(conv1, back_inner)
+    corr1 = back_turns(corr1)
+    back_outer_products(1, 0, corr0)
+    conv1 = back_turns(conv1)
+    conv0 = dot_wide(conv0, back_inner)
+    conv0 = back_turns(conv0)
+    cross1 = dot_wide(cross1, back_inner)
+    back_outer_products(0, 0, conv0)
+    cross1 = back_turns(cross1)
+    back_outer_products(2, 0, cross0)
+    back_outer_products(2, 1, cross1)
+    back_outer_products(0, 1, conv1)
+    back_outer_products(1, 1, corr1)
 
 
 def params(size):

time: 70.2 us -> 70.2 us (level)
  no operation moved by 1% of the time
where the time goes in v7:
time: 70.2 us; the launch traced here: 70 us
  blocking collectives  62.2 us (89%)
  Pallas kernels  7.13 us (10%)
    all_to_all x2, blocking collectives, exchange(): lax.all_to_all(slabs, ALL_AXES, split_axis=0, concat_axis=0, tiled=True)  62.2 us
    pallas_call x1, Pallas kernels, per_device(): pl.pallas_call(functools.partial(convolve_kernel, parts, blocks, per), ou...  4.21 us
    pallas_call x1, Pallas kernels, per_device(): pl.pallas_call(functools.partial(pack_kernel, parts, devices), out_shape=...  1.62 us

profile of v7, /device:TPU:1, one launch (start us, length us, event | category | flops | bytes accessed | tf_op | source)
XLA Modules:
  0.0 70.0 jit_solution(6145826288806357515)
XLA Ops:
  0.6 1.6 %pack.1 = f32[2560,128]{1,0:T(8,128)S(1)} custom-call(bf16[512,256]{1,0:T(8,128)(2,1)} %key_ref.1, bf16[512,256]{1,0:T(8,128)(2,1)} %value_ref.1, bf16[512,256]{1,0:T(8,128)(2,1)} %grad_ref.1, bf16[512,256]{1,0:T(8,128)(2,1)} %query_hbm.1, f32[512,256]{1,0:T(8,128)} %taps_hbm.1), custom_call_target="tpu_custom_call" | custom-call | tf_op jit(solution)/shard_map/pack/pallas_call | solution.py:284
  2.3 0.0 copy-start
  2.3 0.0 copy-start.4
  2.3 33.2 %all_to_all.10 = f32[128,5,4,128]{3,2,1,0:T(4,128)S(1)} all-to-all(f32[128,5,4,128]{3,2,1,0:T(4,128)S(1)} %bitcast.6), channel_id=1, replica_groups=mesh['dp'=2,'outer'=4,'inner'=16] {'dp','outer','inner'}, dimensions={0} | all-to-all | bytes 2621440 | tf_op jit(solution)/shard_map/all_to_all | solution.py:268
  35.4 0.0 copy-done
  35.5 0.0 copy-done.4
  35.5 4.2 %convolve.1 = f32[3072,128]{1,0:T(8,128)S(1)} custom-call(f32[2560,128]{1,0:T(8,128)S(1)} %bitcast.7, bf16[2560,256]{1,0:T(8,128)(2,1)S(1)} %copy-done, f32[2,256,128]{2,1,0:T(8,128)S(1)} %copy-done.4), custom_call_target="tpu_custom_call" | custom-call | tf_op jit(solution)/shard_map/convolve/pallas_call | solution.py:295
  39.7 0.0 copy-start.1
  39.7 0.0 copy-start.2
  39.7 0.0 copy-start.3
  39.7 29.0 %all_to_all.11 = f32[128,6,4,128]{3,2,1,0:T(4,128)S(1)} all-to-all(f32[128,6,4,128]{3,2,1,0:T(4,128)S(1)} %bitcast.5), channel_id=1, replica_groups=mesh['dp'=2,'outer'=4,'inner'=16] {'dp','outer','inner'}, dimensions={0} | all-to-all | bytes 3145728 | tf_op jit(solution)/shard_map/all_to_all | solution.py:268
  68.7 0.0 copy-done.1
  68.7 0.0 copy-done.2
  68.7 0.0 copy-done.3
  68.7 1.3 %unpack.1 = (bf16[512,256]{1,0:T(8,128)(2,1)}, bf16[512,256]{1,0:T(8,128)(2,1)}, bf16[512,256]{1,0:T(8,128)(2,1)}, f32[512,256]{1,0:T(8,128)}) custom-call(f32[3072,128]{1,0:T(8,128)S(1)} %bitcast.4, bf16[512,256]{1,0:T(8,128)(2,1)S(1)} %copy-done.1, bf16[512,256]{1,0:T(8,128)(2,1)S(1)} %copy-done.2, bf16[512,256]{1,0:T(8,128)(2,1)S(1)} %copy-done.3), custom_call_target="tpu_custom_call" | custom-call | tf_op jit(solution)/shard_map/unpack/pallas_call | solution.py:304
Async XLA Ops:
  2.3 33.2 %copy-start = (bf16[2560,256]{1,0:T(8,128)(2,1)S(1)}, bf16[2560,256]{1,0:T(8,128)(2,1)}, u32[]{:S(2)}) copy-start(bf16[2560,256]{1,0:T(8,128)(2,1)} %constant.4.clone.tables_ref) | copy-start | bytes 3932164
  2.3 33.2 %copy-start.4 = (f32[2,256,128]{2,1,0:T(8,128)S(1)}, f32[2,256,128]{2,1,0:T(8,128)}, u32[]{:S(2)}) copy-start(f32[2,256,128]{2,1,0:T(8,128)} %constant.5.clone.twist_ref) | copy-start | bytes 786436
  39.7 29.0 %copy-start.1 = (bf16[512,256]{1,0:T(8,128)(2,1)S(1)}, bf16[512,256]{1,0:T(8,128)(2,1)}, u32[]{:S(2)}) copy-start(bf16[512,256]{1,0:T(8,128)(2,1)} %key_ref.1) | copy-start | bytes 786436
  39.7 29.0 %copy-start.2 = (bf16[512,256]{1,0:T(8,128)(2,1)S(1)}, bf16[512,256]{1,0:T(8,128)(2,1)}, u32[]{:S(2)}) copy-start(bf16[512,256]{1,0:T(8,128)(2,1)} %value_ref.1) | copy-start | bytes 786436
  39.7 29.0 %copy-start.3 = (bf16[512,256]{1,0:T(8,128)(2,1)S(1)}, bf16[512,256]{1,0:T(8,128)(2,1)}, u32[]{:S(2)}) copy-start(bf16[512,256]{1,0:T(8,128)(2,1)} %grad_ref.1) | copy-start | bytes 786436

commit v8 on v4

--- a/solution.py
+++ b/solution.py
@@ -110,15 +110,21 @@
     moves = []
     for piece in range(pieces):
         span = slice(piece * LANES, (piece + 1) * LANES)
-        gq[span, :] = (grad_ref[span, :].astype(jnp.float32) * signal(0, piece)).astype(gq.dtype)
+        here = pl.ds(piece * LANES, LANES)
+
+        def send(n, src, dst):
+            moves.append(pltpu.make_async_copy(src.at[here, :], dst.at[here, :], sems.at[n, piece]))
+            moves[-1].start()
+
+        gf[span, :] = signal(2, piece) * scale
+        send(3, gf, gf_hbm)
         corr = signal(1, piece)
         gk[span, :] = (corr * value_ref[span, :].astype(jnp.float32)).astype(gk.dtype)
+        send(1, gk, gk_hbm)
         gv[span, :] = (corr * key_ref[span, :].astype(jnp.float32)).astype(gv.dtype)
-        gf[span, :] = signal(2, piece) * scale
-        for n, (src, dst) in enumerate(((gq, gq_hbm), (gk, gk_hbm), (gv, gv_hbm), (gf, gf_hbm))):
-            here = pl.ds(piece * LANES, LANES)
-            moves.append(pltpu.make_async_copy(src.at[here, :], dst.at[here, :], sems.at[n, piece]))
-            moves[-1].start()
+        send(2, gv, gv_hbm)
+        gq[span, :] = (grad_ref[span, :].astype(jnp.float32) * signal(0, piece)).astype(gq.dtype)
+        send(0, gq, gq_hbm)
     for move in moves:
         move.wait()
 

time: 70.2 us -> 70.1 us (level)
  no operation moved by 1% of the time
where the time goes in v8:
time: 70.1 us; the launch traced here: 70 us
  blocking collectives  62.2 us (89%)
  Pallas kernels  7.08 us (10%)
    all_to_all x2, blocking collectives, exchange(): lax.all_to_all(slabs, ALL_AXES, split_axis=0, concat_axis=0, tiled=True)  62.2 us
    pallas_call x1, Pallas kernels, per_device(): pl.pallas_call(functools.partial(convolve_kernel, parts, blocks, per), ou...  4.17 us
    pallas_call x1, Pallas kernels, per_device(): pl.pallas_call(functools.partial(pack_kernel, parts, devices), out_shape=...  1.62 us

profile of v8, /device:TPU:1, one launch (start us, length us, event | category | flops | bytes accessed | tf_op | source)
XLA Modules:
  0.0 70.0 jit_solution(12987819670245286884)
XLA Ops:
  0.6 1.6 %pack.1 = f32[2560,128]{1,0:T(8,128)S(1)} custom-call(bf16[512,256]{1,0:T(8,128)(2,1)} %key_ref.1, bf16[512,256]{1,0:T(8,128)(2,1)} %value_ref.1, bf16[512,256]{1,0:T(8,128)(2,1)} %grad_ref.1, bf16[512,256]{1,0:T(8,128)(2,1)} %query_hbm.1, f32[512,256]{1,0:T(8,128)} %taps_hbm.1), custom_call_target="tpu_custom_call" | custom-call | tf_op jit(solution)/shard_map/pack/pallas_call | solution.py:268
  2.3 0.0 copy-start
  2.3 0.0 copy-start.4
  2.3 33.2 %all_to_all.10 = f32[128,5,4,128]{3,2,1,0:T(4,128)S(1)} all-to-all(f32[128,5,4,128]{3,2,1,0:T(4,128)S(1)} %bitcast.6), channel_id=1, replica_groups=mesh['dp'=2,'outer'=4,'inner'=16] {'dp','outer','inner'}, dimensions={0} | all-to-all | bytes 2621440 | tf_op jit(solution)/shard_map/all_to_all | solution.py:252
  35.4 0.0 copy-done
  35.5 0.0 copy-done.4
  35.5 4.2 %convolve.1 = f32[3072,128]{1,0:T(8,128)S(1)} custom-call(f32[2560,128]{1,0:T(8,128)S(1)} %bitcast.7, bf16[2560,256]{1,0:T(8,128)(2,1)S(1)} %copy-done, f32[2,256,128]{2,1,0:T(8,128)S(1)} %copy-done.4), custom_call_target="tpu_custom_call" | custom-call | tf_op jit(solution)/shard_map/convolve/pallas_call | solution.py:279
  39.6 0.0 copy-start.1
  39.6 0.0 copy-start.2
  39.7 0.0 copy-start.3
  39.7 29.0 %all_to_all.11 = f32[128,6,4,128]{3,2,1,0:T(4,128)S(1)} all-to-all(f32[128,6,4,128]{3,2,1,0:T(4,128)S(1)} %bitcast.5), channel_id=1, replica_groups=mesh['dp'=2,'outer'=4,'inner'=16] {'dp','outer','inner'}, dimensions={0} | all-to-all | bytes 3145728 | tf_op jit(solution)/shard_map/all_to_all | solution.py:252
  68.7 0.0 copy-done.1
  68.7 0.0 copy-done.2
  68.7 0.0 copy-done.3
  68.7 1.3 %unpack.1 = (bf16[512,256]{1,0:T(8,128)(2,1)}, bf16[512,256]{1,0:T(8,128)(2,1)}, bf16[512,256]{1,0:T(8,128)(2,1)}, f32[512,256]{1,0:T(8,128)}) custom-call(f32[3072,128]{1,0:T(8,128)S(1)} %bitcast.4, bf16[512,256]{1,0:T(8,128)(2,1)S(1)} %copy-done.1, bf16[512,256]{1,0:T(8,128)(2,1)S(1)} %copy-done.2, bf16[512,256]{1,0:T(8,128)(2,1)S(1)} %copy-done.3), custom_call_target="tpu_custom_call" | custom-call | tf_op jit(solution)/shard_map/unpack/pallas_call | solution.py:288
Async XLA Ops:
  2.3 33.2 %copy-start = (bf16[2560,256]{1,0:T(8,128)(2,1)S(1)}, bf16[2560,256]{1,0:T(8,128)(2,1)}, u32[]{:S(2)}) copy-start(bf16[2560,256]{1,0:T(8,128)(2,1)} %constant.4.clone.tables_ref) | copy-start | bytes 3932164
  2.3 33.2 %copy-start.4 = (f32[2,256,128]{2,1,0:T(8,128)S(1)}, f32[2,256,128]{2,1,0:T(8,128)}, u32[]{:S(2)}) copy-start(f32[2,256,128]{2,1,0:T(8,128)} %constant.5.clone.twist_ref) | copy-start | bytes 786436
  39.6 29.0 %copy-start.1 = (bf16[512,256]{1,0:T(8,128)(2,1)S(1)}, bf16[512,256]{1,0:T(8,128)(2,1)}, u32[]{:S(2)}) copy-start(bf16[512,256]{1,0:T(8,128)(2,1)} %key_ref.1) | copy-start | bytes 786436
  39.6 29.0 %copy-start.2 = (bf16[512,256]{1,0:T(8,128)(2,1)S(1)}, bf16[512,256]{1,0:T(8,128)(2,1)}, u32[]{:S(2)}) copy-start(bf16[512,256]{1,0:T(8,128)(2,1)} %value_ref.1) | copy-start | bytes 786436
  39.7 29.0 %copy-start.3 = (bf16[512,256]{1,0:T(8,128)(2,1)S(1)}, bf16[512,256]{1,0:T(8,128)(2,1)}, u32[]{:S(2)}) copy-start(bf16[512,256]{1,0:T(8,128)(2,1)} %grad_ref.1) | copy-start | bytes 786436
